TPU v7x, 128 devices: a whole 4x4x4 slice. The times are simulated.
128 devices in a mesh: dev: 128 (over y, x, z, core).
Axes of the slice: x: 4, y: 4, z: 4, core: 2. Of those that a mesh axis runs over, the one named last changes fastest.
Arguments:
- right_side: float32 [8192, 3, 128], P('dev'), may hold values from -105 to 105
- vertices: float32 [8192, 3, 128], P('dev'), may hold values from 0 to 1
- panels: int32 [8192, 3, 128], P('dev'), may hold values from 0 to 127
- near_owner: int32 [8192, 2], P('dev'), may hold values from 0 to 127, all different within a row; in each aligned block of 64 rows (0 to 63, 64 to 127, ...) at most 2 rows name the same one
- near_local: int32 [8192, 2], P('dev'), may hold values from 0 to 63
- far_owner: int32 [8192, 2], P('dev'), may hold values from 0 to 127, all different within a row; in each aligned block of 64 rows (0 to 63, 64 to 127, ...) at most 2 rows name the same one
- far_local: int32 [8192, 2], P('dev'), may hold values from 0 to 63
- far_left: float32 [8192, 16, 384], P('dev'), may hold values from -0.5 to 0.5
- far_right: float32 [8192, 16, 384], P('dev'), may hold values from -0.5 to 0.5
Outputs:
- krylov_basis: float32 [2, 8192, 3, 128], P(None, 'dev')
- hessenberg: float32 [3, 2], replicated
Inputs may be any that keep to these rules, and one draw needn't show every extreme that they name: `near_owner`: the two entries of a row differ. Within one device's 64 rows no device number appears more than 2 times, and in every draw some number appears exactly 2 times. `far_owner`: the two entries of a row differ. Within one device's 64 rows no device number appears more than 2 times, and in every draw some number appears exactly 2 times.
All inputs are finite; a program needn't handle non-finite values.
Results may differ from a plain program's by a relative error of at most 0.0003.
Values sent between devices are 32-bit elements; how exact they have to be, the bound alone decides.
A program may use at most 64 MiB of HBM per device.

v0:
```python
import jax
import jax.numpy as jnp
from jax import lax
from jax.sharding import PartitionSpec as P

highest = lax.Precision.HIGHEST
soft_sq = 0.0025
area_floor = 6.25e-06
kelvin_diag = 1.8
norm_eps = 1e-06
barycentric = (
    (2.0 / 3.0, 1.0 / 6.0, 1.0 / 6.0),
    (1.0 / 6.0, 2.0 / 3.0, 1.0 / 6.0),
    (1.0 / 6.0, 1.0 / 6.0, 2.0 / 3.0),
)
index_pairs = ((0, 0), (0, 1), (0, 2), (1, 1), (1, 2), (2, 2))


def panel_corners(vertex_table, connect):
    table_rows = lax.broadcasted_iota(jnp.int32, (vertex_table.shape[1], 1), 0)
    corner_list = []
    for m in range(3):
        select = (table_rows == connect[m][None, :]).astype(jnp.float32)
        corner_list.append(
            jnp.dot(vertex_table, select, precision=highest, preferred_element_type=jnp.float32)
        )
    return jnp.stack(corner_list)


def quad_points(corners):
    edge_one = corners[1] - corners[0]
    edge_two = corners[2] - corners[0]
    cross_x = edge_one[1] * edge_two[2] - edge_one[2] * edge_two[1]
    cross_y = edge_one[2] * edge_two[0] - edge_one[0] * edge_two[2]
    cross_z = edge_one[0] * edge_two[1] - edge_one[1] * edge_two[0]
    weight = jnp.sqrt(cross_x * cross_x + cross_y * cross_y + cross_z * cross_z + area_floor) / 6.0
    points = jnp.stack(
        [
            coords[0] * corners[0] + coords[1] * corners[1] + coords[2] * corners[2]
            for coords in barycentric
        ]
    )
    return (points, weight)


def near_block(points_first, weight_first, points_second, weight_second):
    panel_count = weight_first.shape[0]
    diag_sum = jnp.zeros((panel_count, panel_count), jnp.float32)
    outer_terms = [jnp.zeros((panel_count, panel_count), jnp.float32) for pair_index in index_pairs]
    for s in range(3):
        for t in range(3):
            offset = points_first[s][:, :, None] - points_second[t][:, None, :]
            inverse = lax.rsqrt(
                offset[0] * offset[0] + offset[1] * offset[1] + offset[2] * offset[2] + soft_sq
            )
            diag_sum = diag_sum + inverse
            inverse_cube = inverse * inverse * inverse
            outer_terms = [
                partial_sum + inverse_cube * offset[i] * offset[j]
                for partial_sum, (i, j) in zip(outer_terms, index_pairs)
            ]
    weight_pair = weight_first[:, None] * weight_second[None, :]
    matrix_rows = []
    for i in range(3):
        matrix_row = []
        for j in range(3):
            entry_sum = outer_terms[index_pairs.index((min(i, j), max(i, j)))]
            if i == j:
                entry_sum = entry_sum + kelvin_diag * diag_sum
            matrix_row.append(weight_pair * entry_sum)
        matrix_rows.append(jnp.stack(matrix_row))
    return jnp.stack(matrix_rows)


def apply_near(block_matrix, dense_first, dense_second):
    into_first = jnp.einsum("ijkl,jl->ik", block_matrix, dense_second, precision=highest)
    into_second = jnp.einsum("ijkl,ik->jl", block_matrix, dense_first, precision=highest)
    return (into_first, into_second)


def apply_far(left_factors, right_factors, flat_first, flat_second):
    coef_second = jnp.einsum("frk,fk->fr", right_factors, flat_second, precision=highest)
    into_first = jnp.einsum("frk,fr->fk", left_factors, coef_second, precision=highest)
    coef_first = jnp.einsum("frk,fk->fr", left_factors, flat_first, precision=highest)
    into_second = jnp.einsum("frk,fr->fk", right_factors, coef_first, precision=highest)
    return (into_first, into_second)


def slot_rank(owner_ids):
    entries = owner_ids.shape[0]
    same_owner = owner_ids[:, None] == owner_ids[None, :]
    earlier = lax.broadcasted_iota(jnp.int32, (entries, entries), 1) < lax.broadcasted_iota(
        jnp.int32, (entries, entries), 0
    )
    return jnp.sum(jnp.where(same_owner & earlier, 1, 0), axis=1).astype(jnp.int32)


def per_device(
    right_side, vertices, panels, near_owner, near_local, far_owner, far_local, far_left, far_right
):
    group_size = lax.axis_size("dev")
    clusters_here = right_side.shape[0]
    panel_count = right_side.shape[2]
    near_count = near_owner.shape[0]
    far_count = far_owner.shape[0]
    cap_near = max(2, 4 * near_count // group_size)
    cap_far = max(2, 4 * far_count // group_size)
    slot_count = cap_near + cap_far
    owner_near = near_owner.reshape(-1)
    owner_far = far_owner.reshape(-1)
    rank_near = slot_rank(owner_near)
    flat_near = owner_near * slot_count + rank_near
    flat_far = owner_far * slot_count + cap_near + slot_rank(owner_far)
    corner_slot = owner_near * cap_near + rank_near
    request = jnp.zeros((group_size * slot_count,), jnp.int32)
    request = (
        request.at[flat_near].set(near_local.reshape(-1)).at[flat_far].set(far_local.reshape(-1))
    )
    asked_ids = lax.all_to_all(
        request.reshape(group_size, slot_count), "dev", split_axis=0, concat_axis=0, tiled=True
    )
    asked_near = asked_ids[:, :cap_near]
    one_hot = (
        asked_ids.reshape(-1)[:, None] == lax.broadcasted_iota(jnp.int32, (1, clusters_here), 1)
    ).astype(jnp.float32)
    size_all = float(clusters_here * group_size * 3 * panel_count)

    def near_points(corner_rows):
        flat_corners = corner_rows.reshape((group_size * cap_near,) + corner_rows.shape[2:])
        return jax.vmap(quad_points)(flat_corners[corner_slot])

    corners_here = jax.vmap(panel_corners)(vertices, panels)

    def fetch_data(density):
        received, corner_rows = (
            lax.all_to_all(density[asked_ids], "dev", split_axis=0, concat_axis=0, tiled=True),
            lax.all_to_all(
                corners_here[asked_near], "dev", split_axis=0, concat_axis=0, tiled=True
            ),
        )
        return (received, near_points(corner_rows))

    def product(density):
        received, point_pack = fetch_data(density)
        points_all, weights_all = point_pack
        received_flat = received.reshape(group_size * slot_count, 3, panel_count)
        dense_near = received_flat[flat_near].reshape(near_count, 2, 3, panel_count)
        points_all = points_all.reshape((near_count, 2) + points_all.shape[1:])
        weights_all = weights_all.reshape(near_count, 2, panel_count)
        group_count = near_count // 4

        def grouped(source_array):
            return source_array.reshape((group_count, 4) + source_array.shape[1:])

        def near_group(group_args):
            points_first, weight_first, points_second, weight_second, dense_first, dense_second = (
                group_args
            )
            blocks = jax.vmap(near_block)(points_first, weight_first, points_second, weight_second)
            return jax.vmap(apply_near)(blocks, dense_first, dense_second)

        into_first, into_second = lax.map(
            near_group,
            (
                grouped(points_all[:, 0]),
                grouped(weights_all[:, 0]),
                grouped(points_all[:, 1]),
                grouped(weights_all[:, 1]),
                grouped(dense_near[:, 0]),
                grouped(dense_near[:, 1]),
            ),
        )
        near_terms = jnp.stack(
            [
                into_first.reshape(near_count, 3, panel_count),
                into_second.reshape(near_count, 3, panel_count),
            ],
            axis=1,
        )
        near_terms = near_terms.reshape(2 * near_count, 3, panel_count)
        dense_far = received_flat[flat_far].reshape(far_count, 2, 3 * panel_count)
        far_first, far_second = apply_far(far_left, far_right, dense_far[:, 0], dense_far[:, 1])
        far_terms = jnp.stack([far_first, far_second], axis=1).reshape(
            2 * far_count, 3, panel_count
        )
        outgoing = jnp.zeros((group_size * slot_count, 3, panel_count), jnp.float32)
        outgoing = outgoing.at[flat_near].set(near_terms).at[flat_far].set(far_terms)
        returned = lax.all_to_all(
            outgoing.reshape(group_size, slot_count, 3, panel_count),
            "dev",
            split_axis=0,
            concat_axis=0,
            tiled=True,
        )
        image_sum = jnp.einsum(
            "sc,sk->ck",
            one_hot,
            returned.reshape(group_size * slot_count, 3 * panel_count),
            precision=highest,
        )
        return image_sum.reshape(clusters_here, 3, panel_count)

    def global_mean(pair_list):
        local_sums = jnp.stack([jnp.sum(left_vec * right_vec) for left_vec, right_vec in pair_list])
        return lax.psum(local_sums, "dev") / size_all

    rhs_scale = jnp.sqrt(global_mean([(right_side, right_side)])[0] + norm_eps)
    basis_one = right_side / rhs_scale
    image_one = product(basis_one)
    proj_first = global_mean([(basis_one, image_one)])[0]
    resid_one = image_one - proj_first * basis_one
    norm_first = jnp.sqrt(global_mean([(resid_one, resid_one)])[0] + norm_eps)
    basis_two = resid_one / norm_first
    image_two = product(basis_two)
    proj_cross = global_mean([(basis_one, image_two)])[0]
    partial_resid = image_two - proj_cross * basis_one
    proj_second = global_mean([(basis_two, partial_resid)])[0]
    resid_two = partial_resid - proj_second * basis_two
    norm_second = jnp.sqrt(global_mean([(resid_two, resid_two)])[0] + norm_eps)
    basis_three = resid_two / norm_second
    zero_entry = jnp.zeros((), jnp.float32)
    hessenberg = jnp.stack(
        [
            jnp.stack([proj_first, proj_cross]),
            jnp.stack([norm_first, proj_second]),
            jnp.stack([zero_entry, norm_second]),
        ]
    )
    return (jnp.stack([basis_two, basis_three]), hessenberg)


def solution(mesh):
    in_specs = (
        P("dev", None, None),
        P("dev", None, None),
        P("dev", None, None),
        P("dev", None),
        P("dev", None),
        P("dev", None),
        P("dev", None),
        P("dev", None, None),
        P("dev", None, None),
    )
    out_specs = (P(None, "dev", None, None), P())
    return jax.shard_map(
        per_device, mesh=mesh, in_specs=in_specs, out_specs=out_specs, check_vma=False
    )
```

profile of v0, /device:TPU:1, one launch (start us, length us, event | category | flops | bytes accessed | tf_op | source)
XLA Modules:
  0.0 994.9 jit_solution(2985590609873242473)
XLA Ops:
  9.6 11.5 %all-to-all-start = ((s32[128,1,4]{2,1,0:T(1,128)}), s32[128,1,4]{2,1,0:T(1,128)S(1)}, u32[]{:S(2)}, u32[]{:S(2)}) async-start(s32[128,1,4]{2,1,0:T(1,128)} %bitcast.102), calls=%async_computation | async-start | bytes 131072 | tf_op jit(solution)/shard_map/all_to_all | solution.py:119
  23.0 67.2 %psum.42 = f32[1]{0:T(128)} all-reduce(f32[1]{0:T(128)} %bitcast.131), channel_id=1, replica_groups=mesh['dev'=128] {'dev'}, use_global_device_ids=true, to_apply=%region_5.6 | all-reduce | flops 1 | bytes 8 | tf_op jit(solution)/shard_map/psum | solution.py:205
  96.9 5.7 all-to-all-start.2
  110.2 8.4 all-to-all-done.2
  118.6 6.0 all-to-all-start.1
  145.9 2.8 copy.238
  148.8 3.4 gather_fusion.1
  157.2 197.0 %while.24 = (s32[]{:T(128)}, f32[16,4,3,128]{3,2,1,0:T(4,128)S(1)}, f32[16,4,3,128]{3,2,1,0:T(4,128)}, f32[16,4,128]{2,1,0:T(4,128)}, f32[16,4,128]{2,1,0:T(4,12...) while((s32[]{:T(128)}, f32[16,4,3,128]{3,2,1,0:T(4,128)S(1)}, ...), condition=%wide.region_7.8_spmd, body=%wide.region_6.7_spmd.sunk | while | flops 43057152 | bytes 57729652 | solution.py:162
  357.5 13.3 %scatter_fusion.1 = f32[512,3,128]{2,1,0:T(4,128)} fusion(f32[512,3,128]{2,1,0:T(4,128)} %broadcast.841.clone, s32[128]{0:T(128)S(1)} %get-tuple-element.332, f32[128,3,128]{2,1,0:T(4,128)} %copy.253), kind=kCustom, calls=%fused_computation.10 | custom fusion | bytes 590336 | tf_op jit(solution)/shard_map/scatter | solution.py:187
  370.7 12.6 %scatter_fusion.2 = f32[512,3,128]{2,1,0:T(4,128)} fusion(f32[512,3,128]{2,1,0:T(4,128)} %scatter_fusion.1, s32[128]{0:T(128)S(1)} %fusion.76, f32[128,3,128]{2,1,0:T(4,128)S(1)} %reshape.4437), kind=kCustom, calls=%fused_computation.11 | custom fusion | bytes 590336 | tf_op jit(solution)/shard_map/scatter | solution.py:187
  385.7 10.6 %all-to-all-start.3 = ((f32[128,4,3,128]{3,1,2,0:T(4,128)}), f32[128,4,3,128]{3,1,2,0:T(4,128)}, u32[]{:S(2)}, u32[]{:S(2)}) async-start(f32[128,4,3,128]{3,1,2,0:T(4,128)} %copy.256), calls=%async_computation.3 | async-start | bytes 1572864 | tf_op jit(solution)/shard_map/all_to_all | solution.py:188
  397.8 14.5 %all-to-all-done.3 = f32[128,4,3,128]{3,1,2,0:T(4,128)} async-done(((f32[128,4,3,128]{3,1,2,0:T(4,128)}), f32[128,4,3,128]{3,1,2,0:T(4,128)}, u32[]{:S(2)}, u32[]{:S(2)}) %all-to-all-start.3) | async-done | bytes 786464 | tf_op jit(solution)/shard_map/all_to_all | solution.py:188
  419.2 63.1 %psum.43 = f32[1]{0:T(128)} all-reduce(f32[1]{0:T(128)} %bitcast.157), channel_id=1, replica_groups=mesh['dev'=128] {'dev'}, use_global_device_ids=true, to_apply=%region_11.12 | all-reduce | flops 1 | bytes 8 | tf_op jit(solution)/shard_map/psum | solution.py:205
  483.7 62.6 %psum.44 = f32[1]{0:T(128)} all-reduce(f32[1]{0:T(128)} %bitcast.159), channel_id=1, replica_groups=mesh['dev'=128] {'dev'}, use_global_device_ids=true, to_apply=%region_13.14 | all-reduce | flops 1 | bytes 8 | tf_op jit(solution)/shard_map/psum | solution.py:205
  552.0 21.5 %all_to_all.41 = f32[128,4,3,128]{3,1,2,0:T(4,128)S(1)} all-to-all(f32[128,4,3,128]{3,1,2,0:T(4,128)S(1)} %copy.260), channel_id=1, replica_groups=mesh['dev'=128] {'dev'}, dimensions={0} | all-to-all | bytes 1572864 | tf_op jit(solution)/shard_map/all_to_all | solution.py:136
  579.3 3.2 convolution_bitcast_fusion.1
  584.7 2.8 gather_fusion.6
  590.9 176.3 %while.25 = (s32[]{:T(128)}, f32[16,4,3,128]{3,2,1,0:T(4,128)S(1)}, f32[16,4,3,128]{3,2,1,0:T(4,128)S(1)}, f32[16,4,128]{2,1,0:T(4,128)}, f32[16,4,128]{2,1,0:T(...) while((s32[]{:T(128)}, f32[16,4,3,128]{3,2,1,0:T(4,128)S(1)}, ...), condition=%wide.region_15.16_spmd, body=%wide.region_14.15_spmd.sunk | while | flops 43057152 | bytes 57729144 | solution.py:162
  767.9 4.3 scatter_fusion.3
  772.2 4.3 scatter_fusion.4
  776.8 20.9 %all_to_all.42 = f32[128,4,3,128]{3,1,2,0:T(4,128)S(1)} all-to-all(f32[128,4,3,128]{3,1,2,0:T(4,128)S(1)} %copy.272), channel_id=1, replica_groups=mesh['dev'=128] {'dev'}, dimensions={0} | all-to-all | bytes 1572864 | tf_op jit(solution)/shard_map/all_to_all | solution.py:188
  800.0 63.1 %psum.45 = f32[1]{0:T(128)} all-reduce(f32[1]{0:T(128)} %bitcast.185), channel_id=1, replica_groups=mesh['dev'=128] {'dev'}, use_global_device_ids=true, to_apply=%region_19.20 | all-reduce | flops 1 | bytes 8 | tf_op jit(solution)/shard_map/psum | solution.py:205
  864.5 62.6 %psum.46 = f32[1]{0:T(128)} all-reduce(f32[1]{0:T(128)} %bitcast.187), channel_id=1, replica_groups=mesh['dev'=128] {'dev'}, use_global_device_ids=true, to_apply=%region_21.22 | all-reduce | flops 1 | bytes 8 | tf_op jit(solution)/shard_map/psum | solution.py:205
  928.4 64.1 %psum.47 = f32[1]{0:T(128)} all-reduce(f32[1]{0:T(128)} %bitcast.189), channel_id=1, replica_groups=mesh['dev'=128] {'dev'}, use_global_device_ids=true, to_apply=%region_23.24 | all-reduce | flops 1 | bytes 8 | tf_op jit(solution)/shard_map/psum | solution.py:205
  (758 shorter events, 458.7 us)
Async XLA Ops:
  0.6 137.1 %copy-start = (f32[64,16,384]{2,1,0:T(8,128)S(1)}, f32[64,16,384]{2,1,0:T(8,128)}, u32[]{:S(2)}) copy-start(f32[64,16,384]{2,1,0:T(8,128)} %param.20) | copy-start | bytes 4718596
  0.6 21.7 %copy-start.12 = (s32[64,3,128]{2,0,1:T(8,128)S(1)}, s32[64,3,128]{2,0,1:T(8,128)}, u32[]{:S(2)}) copy-start(s32[64,3,128]{2,0,1:T(8,128)} %param.15) | copy-start | bytes 294916
  0.7 21.7 %copy-start.2 = (f32[64,3,128]{2,0,1:T(8,128)S(1)}, f32[64,3,128]{2,0,1:T(8,128)}, u32[]{:S(2)}) copy-start(f32[64,3,128]{2,0,1:T(8,128)} %param.13) | copy-start | bytes 294916
  0.7 90.2 %copy-start.13 = (f32[64,3,128]{2,0,1:T(8,128)S(1)}, f32[64,3,128]{2,0,1:T(8,128)}, u32[]{:S(2)}) copy-start(f32[64,3,128]{2,0,1:T(8,128)} %param.14) | copy-start | bytes 294916
  9.6 83.9 %all-to-all-start = ((s32[128,1,4]{2,1,0:T(1,128)}), s32[128,1,4]{2,1,0:T(1,128)S(1)}, u32[]{:S(2)}, u32[]{:S(2)}) async-start(s32[128,1,4]{2,1,0:T(1,128)} %bitcast.102), calls=%async_computation | async-start | bytes 131072 | tf_op jit(solution)/shard_map/all_to_all | solution.py:119
  90.9 2.8 copy-start.5
  93.6 13.1 %copy-start.9 = (s32[128,1,4]{2,1,0:T(1,128)}, s32[128,1,4]{2,1,0:T(1,128)S(1)}, u32[]{:S(2)}) copy-start(s32[128,1,4]{2,1,0:T(1,128)S(1)} %all-to-all-done) | copy-start | bytes 6148
  96.9 21.7 %all-to-all-start.2 = ((f32[128,4,3,128]{3,1,2,0:T(4,128)}), f32[128,4,3,128]{3,1,2,0:T(4,128)}, u32[]{:S(2)}, u32[]{:S(2)}) async-start(f32[128,4,3,128]{3,1,2,0:T(4,128)} %copy.244), calls=%async_computation.2 | async-start | bytes 1572864 | tf_op jit(solution)/shard_map/all_to_all | solution.py:136
  118.6 27.3 %all-to-all-start.1 = ((f32[128,2,3,3,128]{4,1,3,2,0:T(2,128)}), f32[128,2,3,3,128]{4,1,3,2,0:T(2,128)}, u32[]{:S(2)}, u32[]{:S(2)}) async-start(f32[128,2,3,3,128]{4,1,3,2,0:T(2,128)} %copy.237), calls=%async_computation.1 | async-start | bytes 2359296 | tf_op jit(solution)/shard_map/all_to_all | solution.py:137
  124.7 6.4 copy-start.1
  383.3 13.5 %copy-start.10 = (s32[128,1,4]{2,1,0:T(1,128)S(1)}, s32[128,1,4]{2,1,0:T(1,128)}, u32[]{:S(2)}) copy-start(s32[128,1,4]{2,1,0:T(1,128)} %copy-done.9) | copy-start | bytes 6148
  385.7 26.5 %all-to-all-start.3 = ((f32[128,4,3,128]{3,1,2,0:T(4,128)}), f32[128,4,3,128]{3,1,2,0:T(4,128)}, u32[]{:S(2)}, u32[]{:S(2)}) async-start(f32[128,4,3,128]{3,1,2,0:T(4,128)} %copy.256), calls=%async_computation.3 | async-start | bytes 1572864 | tf_op jit(solution)/shard_map/all_to_all | solution.py:188
  413.6 3.3 copy-start.6
  414.6 68.4 %copy-start.3 = (f32[64,3,128]{2,0,1:T(8,128)S(1)}, f32[64,3,128]{2,0,1:T(8,128)}, u32[]{:S(2)}) copy-start(f32[64,3,128]{2,0,1:T(8,128)} %param.13) | copy-start | bytes 294916
  419.2 127.6 %copy-start.11 = (f32[64,3,128]{2,0,1:T(8,128)}, f32[64,3,128]{2,0,1:T(8,128)S(1)}, u32[]{:S(2)}) copy-start(f32[64,3,128]{2,0,1:T(8,128)S(1)} %get-tuple-element.334) | copy-start | bytes 294916
  579.3 3.2 copy-start.4
  589.7 1.0 copy-start.8
  798.0 0.9 copy-start.7
where the time goes:
time: 1010 us; the launch traced here: 995 us
  blocking collectives  425 us (42%)
  other arithmetic  194 us (19%)
  local copies, waits for them, and re-layouts  170 us (17%)
  matrix products  141 us (14%)
  starting transfers between devices  33.8 us (3%)
  waiting for transfers between devices  22.9 us (2%)
    psum x6, blocking collectives, global_mean(): return lax.psum(local_sums, 'dev') / size_all  383 us
    mul x192, other arithmetic, near_block(): matrix_row.append(weight_pair * entry_sum)  144 us
    dot_general x32, matrix products, apply_near(): jnp.einsum('ijkl,jl->ik', block_matrix, dense_second, precision=highest)  72.2 us
    dot_general x32, matrix products, apply_near(): jnp.einsum('ijkl,ik->jl', block_matrix, dense_first, precision=highest)  45.4 us
    scatter x4, local copies, waits for them, and re-layouts, product(): outgoing.at[flat_near].set(near_terms).at[flat_far].set(far_terms)  34.5 us
    sub x32, other arithmetic, near_block(): offset = points_first[s][:, :, None] - points_second[t][:, None, :]  30.7 us
    squeeze x32, local copies, waits for them, and re-layouts, product(): lax.map(near_group, (grouped(points_all[:, 0]), grouped(weights_all[:, 0]...  24.3 us
    mul x32, local copies, waits for them, and re-layouts, near_block(): weight_pair = weight_first[:, None] * weight_second[None, :]  22 us
  transfers between devices with their start and end apart: 4, of which 2 were waited for; matrix products, arithmetic and copies ran while one was open for 3% of the time, Pallas kernels for 0%

commit v1 on v0

v1 whole, which is shorter than its diff:
```python
import functools

import jax
import jax.numpy as jnp
from jax import lax
from jax.experimental import pallas as pl
from jax.experimental.pallas import tpu as pltpu
from jax.sharding import PartitionSpec as P

highest = lax.Precision.HIGHEST
soft_sq = 0.0025
area_floor = 6.25e-06
kelvin_diag = 1.8
norm_eps = 1e-06
lanes = 128
f32 = jnp.float32
i32 = jnp.int32
mesh_id = pl.DeviceIdType.MESH


def list_tables(owner_row, local_row):
    shape = (lanes, lanes)
    sub = lax.broadcasted_iota(i32, shape, 0)
    lane = lax.broadcasted_iota(i32, shape, 1)
    sub_f = sub.astype(f32)
    lane_f = lane.astype(f32)
    owner_b = jnp.broadcast_to(owner_row, shape)
    owner_t = owner_b.T
    local_t = jnp.broadcast_to(local_row, shape).T
    same = owner_b == owner_t
    rank_row = jnp.sum(jnp.where(same & (sub < lane), 1.0, 0.0), axis=0, keepdims=True)
    rank_col = jnp.sum(jnp.where(same & (lane < sub), 1.0, 0.0), axis=1, keepdims=True)
    slot_row = owner_row * 2.0 + rank_row
    requests, entries = [], []
    for k in range(2):
        hit = (owner_t == lane_f) & (rank_col == float(k))
        requests.append(jnp.sum(jnp.where(hit, local_t, 0.0), axis=0, keepdims=True))
        entries.append(
            jnp.sum(jnp.where(hit, sub_f - float(lanes), 0.0), axis=0, keepdims=True) + float(lanes)
        )
    return slot_row, requests, entries


def kernel(
    n,
    near,
    far,
    index_ref,
    x_ref,
    vert_ref,
    panel_ref,
    left_ref,
    right_ref,
    basis_ref,
    hess_ref,
    req_send,
    req_recv,
    tab_v,
    tab_s,
    ask_v,
    ask_s,
    one_hot,
    panel_f,
    geo_send,
    geo_recv,
    x_send,
    x_recv,
    y_send,
    y_recv,
    near_send,
    near_recv,
    far_send,
    far_recv,
    points,
    points_t,
    blocks,
    first_rows,
    first_cols,
    out_cols,
    near_terms,
    far_terms,
    y_here,
    z_here,
    sum_send,
    sum_recv,
    send_sem,
    recv_sem,
    local_sem,
):
    me = lax.axis_index("dev")
    clusters = x_ref.shape[0]
    size_all = float(clusters * n * 3 * lanes)

    barrier = pltpu.get_barrier_semaphore()

    def greet(i, carry):
        pl.semaphore_signal(
            barrier, inc=1, device_id=(lax.rem(me + i, n),), device_id_type=mesh_id
        )
        return carry

    lax.fori_loop(1, n, greet, 0)

    def asked_id(k, o):
        return jnp.clip(ask_s[k, o], 0, clusters - 1)

    def entry_slot(row, e):
        slot = jnp.clip(tab_s[row, e], 0, 2 * n - 1)
        return slot >> 1, slot & 1

    index_rows = index_ref[...].astype(f32)
    near_slot, near_req, near_entry = list_tables(index_rows[0:1], index_rows[1:2])
    far_slot, far_req, far_entry = list_tables(index_rows[2:3], index_rows[3:4])
    rows = [near_slot, far_slot] + near_entry + far_entry
    tab_v[...] = jnp.concatenate(rows + [jnp.zeros((2, lanes), f32)], axis=0).astype(i32)
    to_smem = pltpu.make_async_copy(tab_v, tab_s, local_sem.at[0])
    to_smem.start()
    req_rows = jnp.concatenate(near_req + far_req + [jnp.zeros((lanes - 4, lanes), f32)], axis=0)
    req_send[...] = req_rows.T[:n].reshape(n, 1, lanes)
    panel_f[...] = panel_ref[...].astype(f32)
    near_terms[pl.ds(4 * lanes, 8), :] = jnp.zeros((8, lanes), f32)
    far_terms[pl.ds(4 * lanes, 8), :] = jnp.zeros((8, lanes), f32)
    out_cols[...] = jnp.zeros(out_cols.shape, f32)

    pl.semaphore_wait(barrier, n - 1)

    def exchange(send, recv, which, fill):
        fill(me)
        pltpu.make_async_copy(send.at[me], recv.at[me], recv_sem.at[which]).start()

        def step(i, carry):
            peer = lax.rem(me + i, n)
            fill(peer)
            pltpu.make_async_remote_copy(
                send.at[peer],
                recv.at[me],
                send_sem.at[which],
                recv_sem.at[which],
                device_id=(peer,),
                device_id_type=mesh_id,
            ).start()
            return carry

        lax.fori_loop(1, n, step, 0)

    def arrived(recv, which):
        pltpu.make_async_copy(recv, recv, recv_sem.at[which]).wait()

    def sent(send, which):
        part = send.at[pl.ds(0, n - 1)]
        pltpu.make_async_copy(part, part, send_sem.at[which]).wait()

    exchange(req_send, req_recv, 0, lambda o: None)
    arrived(req_recv, 0)
    asked = req_recv[...].reshape(n, lanes)
    if n < lanes:
        asked = jnp.concatenate([asked, jnp.zeros((lanes - n, lanes), f32)], axis=0)
    asked = asked.T
    ask_v[...] = asked[0:8].astype(i32)
    ask_copy = pltpu.make_async_copy(ask_v, ask_s, local_sem.at[1])
    ask_copy.start()
    cluster_ids = lax.broadcasted_iota(i32, (clusters, lanes), 0).astype(f32)
    for k in range(4):
        one_hot[k] = jnp.where(cluster_ids == asked[k : k + 1], 1.0, 0.0)
    ask_copy.wait()
    to_smem.wait()

    def fill_geo(o):
        for k in range(2):
            c = asked_id(k, o)
            geo_send[o, k, 0] = vert_ref[c]
            geo_send[o, k, 1] = panel_f[c]

    def fill_density(send, source):
        def fill(o):
            for k in range(4):
                send[o, k] = source[asked_id(k, o)]

        return fill

    exchange(geo_send, geo_recv, 1, fill_geo)
    exchange(x_send, x_recv, 2, fill_density(x_send, x_ref))
    arrived(geo_recv, 1)

    def make_points(p, carry):
        owner_a, rank_a = entry_slot(0, p)
        owner_b, rank_b = entry_slot(0, near + p)
        va = geo_recv[owner_a, rank_a, 0]
        vb = geo_recv[owner_b, rank_b, 0]
        pa = geo_recv[owner_a, rank_a, 1].astype(i32)
        pb = geo_recv[owner_b, rank_b, 1].astype(i32)
        table = jnp.concatenate([va, va[0:1], vb, vb[0:1]], axis=0)
        corners = []
        for m in range(3):
            picks = jnp.concatenate(
                [
                    jnp.broadcast_to(pa[m : m + 1], (4, lanes)),
                    jnp.broadcast_to(pb[m : m + 1], (4, lanes)),
                ],
                axis=0,
            )
            corners.append(
                jnp.take_along_axis(table, picks, axis=1, mode="promise_in_bounds")
            )
        edge_one = corners[1] - corners[0]
        edge_two = corners[2] - corners[0]
        cross = edge_one * pltpu.roll(edge_two, 7, 0) - pltpu.roll(edge_one, 7, 0) * edge_two
        squares = cross * cross
        area = squares + pltpu.roll(squares, 7, 0) + pltpu.roll(squares, 6, 0)
        weight = jnp.sqrt(area + area_floor) / 6.0
        for s in range(3):
            others = [corners[m] for m in range(3) if m != s]
            points[p, s] = (2.0 / 3.0) * corners[s] + (1.0 / 6.0) * (others[0] + others[1])
        points[p, 3] = weight
        return carry

    lax.fori_loop(0, near, make_points, 0)

    def turn_points(g, carry):
        points_t[g] = points[pl.ds(4 * g, 4)].reshape(lanes, lanes).T
        return carry

    lax.fori_loop(0, near // 4, turn_points, 0)

    chunk = 16

    def make_block(p, carry):
        group = p // 4
        shift = lanes - (p % 4) * 32
        for c in range(lanes // chunk):
            at = pltpu.roll(points_t[group, pl.ds(c * chunk, chunk), :], shift, 1)
            inv_sum = jnp.zeros((chunk, lanes), f32)
            cube_sum = jnp.zeros((chunk, lanes), f32)
            outer = [jnp.zeros((chunk, lanes), f32) for _ in range(5)]
            for s in range(3):
                a = [at[:, 8 * s + i : 8 * s + i + 1] for i in range(3)]
                for t in range(3):
                    d = [a[i] - points[p, t, 4 + i : 5 + i, :] for i in range(3)]
                    inv = lax.rsqrt(d[0] * d[0] + d[1] * d[1] + (d[2] * d[2] + soft_sq))
                    cube = inv * inv * inv
                    e0 = cube * d[0]
                    e1 = cube * d[1]
                    inv_sum = inv_sum + inv
                    cube_sum = cube_sum + cube
                    outer = [
                        outer[0] + e0 * d[0],
                        outer[1] + e0 * d[1],
                        outer[2] + e0 * d[2],
                        outer[3] + e1 * d[1],
                        outer[4] + e1 * d[2],
                    ]
            weight = at[:, 24:25] * points[p, 3, 4:5, :]
            last = inv_sum - soft_sq * cube_sum - outer[0] - outer[3]
            diag = kelvin_diag * inv_sum
            at_rows = pl.ds(c * chunk, chunk)
            blocks[p, 0, at_rows, :] = weight * (outer[0] + diag)
            blocks[p, 1, at_rows, :] = weight * outer[1]
            blocks[p, 2, at_rows, :] = weight * outer[2]
            blocks[p, 3, at_rows, :] = weight * (outer[3] + diag)
            blocks[p, 4, at_rows, :] = weight * outer[4]
            blocks[p, 5, at_rows, :] = weight * (last + diag)
        return carry

    pair_at = ((0, 1, 2), (1, 3, 4), (2, 4, 5))

    def apply_far(recv):
        def step(f, carry):
            owner_a, rank_a = entry_slot(1, f)
            owner_b, rank_b = entry_slot(1, far + f)
            xa = recv[owner_a, 2 + rank_a]
            xb = recv[owner_b, 2 + rank_b]
            left = [left_ref[f, :, pl.ds(c * lanes, lanes)] for c in range(3)]
            right = [right_ref[f, :, pl.ds(c * lanes, lanes)] for c in range(3)]
            coef_b = jnp.sum(
                right[0] * xb[0:1] + right[1] * xb[1:2] + right[2] * xb[2:3], axis=1, keepdims=True
            )
            coef_a = jnp.sum(
                left[0] * xa[0:1] + left[1] * xa[1:2] + left[2] * xa[2:3], axis=1, keepdims=True
            )
            for c in range(3):
                far_terms[pl.ds(4 * f + c, 1), :] = jnp.sum(left[c] * coef_b, axis=0, keepdims=True)
                far_terms[pl.ds(4 * (far + f) + c, 1), :] = jnp.sum(
                    right[c] * coef_a, axis=0, keepdims=True
                )
            return carry

        lax.fori_loop(0, far, step, 0)

    per_tile = lanes // 4
    tiles = -(-near // per_tile)

    def apply_near(recv):
        def gather(h, carry):
            parts = []
            for q in range(2):
                owner, rank = entry_slot(0, 2 * h + q)
                rows_q = recv[owner, rank]
                parts += [rows_q, rows_q[0:1]]
            first_rows[pl.ds(pl.multiple_of(8 * h, 8), 8), :] = jnp.concatenate(parts, axis=0)
            return carry

        lax.fori_loop(0, near // 2, gather, 0)
        for g in range(tiles):
            first_cols[g] = first_rows[pl.ds(g * lanes, lanes), :].T
        lane_ids = lax.broadcasted_iota(i32, (chunk, lanes), 1)

        def step(p, carry):
            group = p // per_tile
            base = 4 * (p % per_tile)
            owner_b, rank_b = entry_slot(0, near + p)
            xb = recv[owner_b, rank_b]
            into = [jnp.zeros((chunk, lanes), f32) for _ in range(3)]
            for c in range(lanes // chunk):
                at_rows = pl.ds(c * chunk, chunk)
                cols = pltpu.roll(first_cols[group, at_rows, :], lanes - base, 1)
                mats = [blocks[p, q, at_rows, :] for q in range(6)]
                kept = out_cols[group, at_rows, :]
                for i in range(3):
                    m = [mats[q] for q in pair_at[i]]
                    summed = jnp.sum(
                        m[0] * xb[0:1] + m[1] * xb[1:2] + m[2] * xb[2:3], axis=1, keepdims=True
                    )
                    kept = jnp.where(lane_ids == base + i, summed, kept)
                    xa = cols[:, i : i + 1]
                    into = [into[j] + m[j] * xa for j in range(3)]
                out_cols[group, at_rows, :] = kept
            for j in range(3):
                near_terms[pl.ds(4 * (near + p) + j, 1), :] = jnp.sum(
                    into[j], axis=0, keepdims=True
                )
            return carry

        lax.fori_loop(0, near, step, 0)
        for g in range(tiles):
            count = min(lanes, 4 * near - g * lanes)
            near_terms[pl.ds(g * lanes, count), :] = out_cols[g].T[:count]

    def fill_terms(send, source, row):
        def fill(o):
            for k in range(2):
                entry = jnp.clip(tab_s[row + k, o], 0, lanes)
                send[o, k] = source[pl.ds(4 * entry, 3), :]

        return fill

    def reduce_terms(stage, target):
        for c in range(3):
            total = jnp.zeros((clusters, lanes), f32)
            for k in range(2):
                total = total + jnp.dot(
                    one_hot[k, :, pl.ds(0, n)],
                    near_recv[stage, :, k, c, :],
                    precision=highest,
                    preferred_element_type=f32,
                )
                total = total + jnp.dot(
                    one_hot[2 + k, :, pl.ds(0, n)],
                    far_recv[stage, :, k, c, :],
                    precision=highest,
                    preferred_element_type=f32,
                )
            target[:, c, :] = total

    def mean_of(u, v):
        return jnp.sum(jnp.sum(u * v, axis=0), keepdims=True) * (1.0 / size_all)

    def send_sums(which, values):
        lane_row = lax.broadcasted_iota(i32, (1, lanes), 1)
        row = jnp.zeros((1, lanes), f32)
        for j, value in enumerate(values):
            row = jnp.where(lane_row == j, value, row)
        sum_send[which] = row
        pltpu.make_async_copy(
            sum_send.at[which], sum_recv.at[which, me], recv_sem.at[7 + which]
        ).start()

        def step(i, carry):
            peer = lax.rem(me + i, n)
            pltpu.make_async_remote_copy(
                sum_send.at[which],
                sum_recv.at[which, me],
                send_sem.at[7 + which],
                recv_sem.at[7 + which],
                device_id=(peer,),
                device_id_type=mesh_id,
            ).start()
            return carry

        lax.fori_loop(1, n, step, 0)

    def take_sums(which, count):
        arrived(sum_recv.at[which], 7 + which)
        total = jnp.sum(sum_recv[which], axis=0)
        return [total[0:1, j : j + 1] for j in range(count)]

    half = near // 2
    lax.fori_loop(0, half, make_block, 0)
    arrived(x_recv, 2)
    apply_far(x_recv)
    exchange(far_send.at[0], far_recv.at[0], 3, fill_terms(far_send.at[0], far_terms, 4))
    lax.fori_loop(half, near, make_block, 0)
    apply_near(x_recv)
    exchange(near_send.at[0], near_recv.at[0], 4, fill_terms(near_send.at[0], near_terms, 2))
    arrived(far_recv.at[0], 3)
    arrived(near_recv.at[0], 4)
    reduce_terms(0, y_here)

    exchange(y_send, y_recv, 9, fill_density(y_send, y_here))
    x = x_ref[...]
    y = y_here[...]
    send_sums(0, [mean_of(x, x), mean_of(x, y), mean_of(y, y)])
    arrived(y_recv, 9)
    apply_far(y_recv)
    exchange(far_send.at[1], far_recv.at[1], 5, fill_terms(far_send.at[1], far_terms, 4))
    apply_near(y_recv)
    exchange(near_send.at[1], near_recv.at[1], 6, fill_terms(near_send.at[1], near_terms, 2))
    xx, xy, yy = take_sums(0, 3)
    scale_sq = xx + norm_eps
    scale = jnp.sqrt(scale_sq)
    proj_first = xy / scale_sq
    resid_sq = (yy - proj_first * xy * (1.0 + norm_eps / scale_sq)) / scale_sq
    norm_sq = resid_sq + norm_eps
    norm_first = jnp.sqrt(norm_sq)
    shrink = 1.0 / (scale * norm_first)
    x = x_ref[...]
    y = y_here[...]
    basis_one = x / scale
    basis_two = (y - proj_first * x) * shrink
    basis_ref[0] = basis_two
    arrived(far_recv.at[1], 5)
    arrived(near_recv.at[1], 6)
    reduce_terms(1, z_here)
    image_two = (z_here[...] - proj_first * y_here[...]) * shrink
    send_sums(
        1, [mean_of(basis_one, image_two), mean_of(basis_two, image_two), mean_of(image_two, image_two)]
    )
    cross, second, image_sq = take_sums(1, 3)
    one_sq = xx / scale_sq
    two_sq = resid_sq / norm_sq
    one_two = xy * norm_eps / (scale_sq * scale_sq * norm_first)
    last_sq = (
        image_sq
        + cross * cross * (one_sq - 2.0)
        + second * second * (two_sq - 2.0)
        + 2.0 * cross * second * one_two
    )
    norm_second = jnp.sqrt(last_sq + norm_eps)
    shrink_two = 1.0 / norm_second
    basis_ref[1] = (image_two - cross * basis_one - second * basis_two) * shrink_two
    row_id = lax.broadcasted_iota(i32, (3, 2), 0)
    col_id = lax.broadcasted_iota(i32, (3, 2), 1)
    hess = jnp.zeros((3, 2), f32)
    placed = (
        (0, 0, proj_first),
        (0, 1, cross),
        (1, 0, norm_first),
        (1, 1, second),
        (2, 1, norm_second),
    )
    for r, c, value in placed:
        hess = jnp.where((row_id == r) & (col_id == c), value, hess)
    hess_ref[...] = hess

    sent(req_send, 0)
    sent(geo_send, 1)
    sent(x_send, 2)
    sent(far_send.at[0], 3)
    sent(near_send.at[0], 4)
    sent(far_send.at[1], 5)
    sent(near_send.at[1], 6)
    sent(y_send, 9)
    for which in range(2):
        sent(sum_recv.at[which], 7 + which)


def per_device(
    right_side, vertices, panels, near_owner, near_local, far_owner, far_local, far_left, far_right
):
    n = lax.axis_size("dev")
    near = near_owner.shape[0]
    far = far_owner.shape[0]
    clusters = right_side.shape[0]

    def entry_row(table, fill):
        row = table.T.reshape(1, -1)
        return jnp.pad(row, ((0, 0), (0, lanes - row.shape[1])), constant_values=fill)

    index = jnp.concatenate(
        [
            entry_row(near_owner, -1),
            entry_row(near_local, 0),
            entry_row(far_owner, -1),
            entry_row(far_local, 0),
        ]
        * 2,
        axis=0,
    )
    tiles = -(-4 * near // lanes)
    vmem = pltpu.VMEM
    return pl.pallas_call(
        functools.partial(kernel, n, near, far),
        out_shape=(
            jax.ShapeDtypeStruct((2, clusters, 3, lanes), f32),
            jax.ShapeDtypeStruct((3, 2), f32),
        ),
        in_specs=[pl.BlockSpec(memory_space=vmem)] * 6,
        out_specs=(pl.BlockSpec(memory_space=vmem),) * 2,
        scratch_shapes=[
            vmem((n, 1, lanes), f32),
            vmem((n, 1, lanes), f32),
            vmem((8, lanes), i32),
            pltpu.SMEM((8, lanes), i32),
            vmem((8, lanes), i32),
            pltpu.SMEM((8, lanes), i32),
            vmem((4, clusters, lanes), f32),
            vmem((clusters, 3, lanes), f32),
            vmem((n, 2, 2, 3, lanes), f32),
            vmem((n, 2, 2, 3, lanes), f32),
            vmem((n, 4, 3, lanes), f32),
            vmem((n, 4, 3, lanes), f32),
            vmem((n, 4, 3, lanes), f32),
            vmem((n, 4, 3, lanes), f32),
            vmem((2, n, 2, 3, lanes), f32),
            vmem((2, n, 2, 3, lanes), f32),
            vmem((2, n, 2, 3, lanes), f32),
            vmem((2, n, 2, 3, lanes), f32),
            vmem((near, 4, 8, lanes), f32),
            vmem((near // 4, lanes, lanes), f32),
            vmem((near, 6, lanes, lanes), f32),
            vmem((tiles * lanes, lanes), f32),
            vmem((tiles, lanes, lanes), f32),
            vmem((tiles, lanes, lanes), f32),
            vmem((4 * lanes + 8, lanes), f32),
            vmem((4 * lanes + 8, lanes), f32),
            vmem((clusters, 3, lanes), f32),
            vmem((clusters, 3, lanes), f32),
            vmem((2, 1, lanes), f32),
            vmem((2, n, 1, lanes), f32),
            pltpu.SemaphoreType.DMA((10,)),
            pltpu.SemaphoreType.DMA((10,)),
            pltpu.SemaphoreType.DMA((2,)),
        ],
        compiler_params=pltpu.CompilerParams(
            collective_id=0, has_side_effects=True, vmem_limit_bytes=58 * 1024 * 1024
        ),
    )(index, right_side, vertices, panels, far_left, far_right)


def solution(mesh):
    block = P("dev", None, None)
    pair = P("dev", None)
    return jax.shard_map(
        per_device,
        mesh=mesh,
        in_specs=(block, block, block, pair, pair, pair, pair, block, block),
        out_specs=(P(None, "dev", None, None), P()),
        check_vma=False,
    )
```

time: 1010 us -> 244 us (0.24); the launches traced: 995 us -> 244 us
  blocking collectives: 425 us -> 0 us
  Pallas kernels: 0 us -> 232 us
  other arithmetic: 194 us -> 0 us
  local copies, waits for them, and re-layouts: 170 us -> 11.4 us
  matrix products: 141 us -> 0 us
  starting transfers between devices: 33.8 us -> 0 us
  waiting for transfers between devices: 22.9 us -> 0 us
    psum x6 -> x0, blocking collectives: 383 us -> none  [global_mean(): return lax.psum(local_sums, 'dev') / size_all]
    pallas_call x0 -> x1, Pallas kernels: none -> 232 us  [per_device(): pl.pallas_call(functools.partial(kernel, n, near, far), out_shape=(jax.Sh...]
    mul x193 -> x0, other arithmetic: 145 us -> none  [the longest x192 144 us: near_block(): matrix_row.append(weight_pair * entry_sum)]
    dot_general x77 -> x0, matrix products: 141 us -> none  [the longest x32 72.2 us: apply_near(): jnp.einsum('ijkl,jl->ik', block_matrix, dense_second, precision=highest)]
    all_to_all x2 -> x0, blocking collectives: 42.4 us -> none  [the longest x1 21.5 us: fetch_data(): lax.all_to_all(density[asked_ids], 'dev', split_axis=0, concat_axis=0, ti...]
    scatter x6 -> x0, local copies, waits for them, and re-layouts: 36.4 us -> none  [the longest x4 34.5 us: product(): outgoing.at[flat_near].set(near_terms).at[flat_far].set(far_terms)]
    all_to_all x4 -> x0, starting transfers between devices: 33.8 us -> none  [the longest x1 11.5 us: per_device(): lax.all_to_all(request.reshape(group_size, slot_count), 'dev', split_axis...]
    sub x32 -> x0, other arithmetic: 30.7 us -> none  [near_block(): offset = points_first[s][:, :, None] - points_second[t][:, None, :]]
  transfers between devices with their start and end apart: 4 -> 0, of which waited for: 2 -> 0; matrix products, arithmetic and copies ran while one was open for 3% -> 0% of each run, Pallas kernels for 0% -> 0%
where the time goes in v1:
time: 244 us
  Pallas kernels  232 us (95%)
  local copies, waits for them, and re-layouts  11.4 us (5%)
    pallas_call x1, Pallas kernels, per_device(): pl.pallas_call(functools.partial(kernel, n, near, far), out_shape=(jax.Sh...  232 us

profile of v1, /device:TPU:1, one launch (start us, length us, event | category | flops | bytes accessed | tf_op | source)
XLA Modules:
  0.0 243.9 jit_solution(7130877983807865185)
XLA Ops:
  0.6 0.8 reshape.16
  1.4 0.8 reshape.17
  2.1 0.8 reshape.18
  2.9 0.8 reshape.19
  3.7 0.6 concatenate.3.index_ref
  4.3 1.6 copy.11.x_ref
  5.9 1.6 copy.12.vert_ref
  7.5 1.6 copy.13.panel_ref
  9.1 231.8 %shard_map.104 = (f32[2,64,3,128]{3,2,1,0:T(4,128)}, f32[3,2]{1,0:T(4,128)}) custom-call(s32[8,128]{1,0:T(8,128)} %concatenate.3.index_ref, f32[64,3,128]{2,1,0:T(4,128)} %copy.11.x_ref, f32[64,3,128]{2,1,0:T(4,128)} %copy.12.vert_ref, s32[64,3,128]{2,1,0:T(4,128)} %copy.13.panel_ref, f32[64,16,384]{2,1,0:T(8,128)} %left_ref.1, f32[64,16,384]{2,1,0:T(8,128)} %right_ref.1), custom_call_target="tpu_custom_call" | custom-call | tf_op jit(solution)/shard_map/pallas_call | solution.py:500
  240.9 1.6 copy.14
  242.6 1.3 copy.15

commit v2 on v1

v2 whole, which is shorter than its diff:
```python
import functools

import jax
import jax.numpy as jnp
from jax import lax
from jax.experimental import pallas as pl
from jax.experimental.pallas import tpu as pltpu
from jax.sharding import PartitionSpec as P

highest = lax.Precision.HIGHEST
soft_sq = 0.0025
area_floor = 6.25e-06
kelvin_diag = 1.8
norm_eps = 1e-06
lanes = 128
f32 = jnp.float32
i32 = jnp.int32
bf16 = jnp.bfloat16
mesh_id = pl.DeviceIdType.MESH


def list_tables(owners, locals_, count):
    owner_row = jnp.concatenate([owners[0:1], owners[1:2]], axis=1).astype(f32)
    local_row = jnp.concatenate([locals_[0:1], locals_[1:2]], axis=1).astype(f32)
    shape = (lanes, lanes)
    sub = lax.broadcasted_iota(i32, shape, 0)
    lane = lax.broadcasted_iota(i32, shape, 1)
    tile = (2 * (sub % count) + sub // count - lanes).astype(f32)
    lane_f = lane.astype(f32)
    owner_b = jnp.broadcast_to(owner_row, shape)
    owner_t = owner_b.T
    local_t = jnp.broadcast_to(local_row, shape).T
    same = owner_b == owner_t
    rank_row = jnp.sum(jnp.where(same & (sub < lane), 1.0, 0.0), axis=0, keepdims=True)
    rank_col = jnp.sum(jnp.where(same & (lane < sub), 1.0, 0.0), axis=1, keepdims=True)
    slot_row = owner_row * 2.0 + rank_row
    requests, entries = [], []
    for k in range(2):
        hit = (owner_t == lane_f) & (rank_col == float(k))
        requests.append(jnp.sum(jnp.where(hit, local_t, 0.0), axis=0, keepdims=True))
        entries.append(
            jnp.sum(jnp.where(hit, tile, 0.0), axis=0, keepdims=True) + float(lanes)
        )
    return slot_row, requests, entries


def three_parts(rows):
    high = rows.astype(bf16).astype(f32)
    rest = rows - high
    middle = rest.astype(bf16).astype(f32)
    return [high, middle, rest - middle]


def kernel(
    n,
    near,
    far,
    near_owner_ref,
    near_local_ref,
    far_owner_ref,
    far_local_ref,
    x_ref,
    vert_ref,
    panel_ref,
    left_ref,
    right_ref,
    basis_ref,
    hess_ref,
    req_send,
    req_recv,
    tab_v,
    tab_s,
    ask_v,
    ask_s,
    one_hot,
    x_here,
    vert_here,
    panel_here,
    geo_send,
    geo_recv,
    x_send,
    x_recv,
    yn_send,
    yn_recv,
    yf_send,
    yf_recv,
    near_send,
    near_recv,
    far_send,
    far_recv,
    points,
    first_rows,
    first_cols,
    picker,
    cols_even,
    cols_odd,
    blocks_0,
    blocks_1,
    blocks_2,
    blocks_3,
    near_terms,
    far_terms,
    y_all,
    z_all,
    y_here,
    sum_send,
    sum_recv,
    send_sem,
    recv_sem,
    local_sem,
):
    me = lax.axis_index("dev")
    clusters = x_ref.shape[1]
    blocks = (blocks_0, blocks_1, blocks_2, blocks_3)
    size_all = float(clusters * n * 3 * lanes)

    barrier = pltpu.get_barrier_semaphore()

    def greet(i, carry):
        pl.semaphore_signal(
            barrier, inc=1, device_id=(lax.rem(me + i, n),), device_id_type=mesh_id
        )
        return carry

    lax.fori_loop(1, n, greet, 0)

    def asked_id(k, o):
        return jnp.clip(ask_s[k, o], 0, clusters - 1)

    def entry_slot(row, e):
        slot = jnp.clip(tab_s[row, e], 0, 2 * n - 1)
        return slot >> 1, slot & 1

    near_slot, near_req, near_entry = list_tables(near_owner_ref[...], near_local_ref[...], near)
    far_slot, far_req, far_entry = list_tables(far_owner_ref[...], far_local_ref[...], far)
    rows = [near_slot, far_slot] + near_entry + far_entry
    tab_v[...] = jnp.concatenate(rows + [jnp.zeros((2, lanes), f32)], axis=0).astype(i32)
    to_smem = pltpu.make_async_copy(tab_v, tab_s, local_sem.at[0])
    to_smem.start()
    req_rows = jnp.concatenate(near_req + far_req + [jnp.zeros((lanes - 4, lanes), f32)], axis=0)
    req_send[...] = req_rows.T[:n].reshape(n, 1, lanes)
    for c in range(3):
        x_here[:, c, :] = x_ref[c]
        vert_here[:, c, :] = vert_ref[c]
        panel_here[:, c, :] = panel_ref[c].astype(f32)
    near_terms[pl.ds(4 * lanes, 8), :] = jnp.zeros((8, lanes), f32)
    far_terms[pl.ds(4 * lanes, 8), :] = jnp.zeros((8, lanes), f32)

    picked = lax.broadcasted_iota(i32, (lanes, lanes), 0)
    for r in range(4):
        for j in range(9):
            place = picked - 32 * r
            if j < 8:
                hit = (place == j) | (place == 8 + j) | (place == 16 + j)
            else:
                hit = (place >= 24) & (place < 27)
            picker[r, :, pl.ds(j * lanes, lanes)] = jnp.where(hit, 1.0, 0.0).astype(bf16)

    pl.semaphore_wait(barrier, n - 1)

    def exchange(send, recv, which, fill):
        fill(me)
        pltpu.make_async_copy(send.at[me], recv.at[me], recv_sem.at[which]).start()

        def step(i, carry):
            peer = lax.rem(me + i, n)
            fill(peer)
            pltpu.make_async_remote_copy(
                send.at[peer],
                recv.at[me],
                send_sem.at[which],
                recv_sem.at[which],
                device_id=(peer,),
                device_id_type=mesh_id,
            ).start()
            return carry

        lax.fori_loop(1, n, step, 0)

    def arrived(recv, which):
        pltpu.make_async_copy(recv, recv, recv_sem.at[which]).wait()

    def sent(send, which):
        part = send.at[pl.ds(0, n - 1)]
        pltpu.make_async_copy(part, part, send_sem.at[which]).wait()

    exchange(req_send, req_recv, 0, lambda o: None)
    arrived(req_recv, 0)
    asked = req_recv[...].reshape(n, lanes)
    if n < lanes:
        asked = jnp.concatenate([asked, jnp.zeros((lanes - n, lanes), f32)], axis=0)
    asked = asked.T
    ask_v[...] = asked[0:8].astype(i32)
    ask_copy = pltpu.make_async_copy(ask_v, ask_s, local_sem.at[1])
    ask_copy.start()
    cluster_ids = lax.broadcasted_iota(i32, (clusters, lanes), 0).astype(f32)
    for k in range(4):
        one_hot[k] = jnp.where(cluster_ids == asked[k : k + 1], 1.0, 0.0)
    ask_copy.wait()
    to_smem.wait()

    def fill_geo(o):
        for k in range(2):
            c = asked_id(k, o)
            geo_send[o, k, 0] = vert_here[c]
            geo_send[o, k, 1] = panel_here[c]

    def fill_density(send, source, slots):
        def fill(o):
            for j, k in enumerate(slots):
                send[o, j] = source[asked_id(k, o)]

        return fill

    exchange(geo_send, geo_recv, 1, fill_geo)
    exchange(x_send, x_recv, 2, fill_density(x_send, x_here, (0, 1, 2, 3)))
    arrived(geo_recv, 1)

    def make_points(p):
        owner_a, rank_a = entry_slot(0, p)
        owner_b, rank_b = entry_slot(0, near + p)
        va = geo_recv[owner_a, rank_a, 0]
        vb = geo_recv[owner_b, rank_b, 0]
        pa = geo_recv[owner_a, rank_a, 1].astype(i32)
        pb = geo_recv[owner_b, rank_b, 1].astype(i32)
        table = jnp.concatenate([va, va[0:1], vb, vb[0:1]], axis=0)
        corners = []
        for m in range(3):
            picks = jnp.concatenate(
                [
                    jnp.broadcast_to(pa[m : m + 1], (4, lanes)),
                    jnp.broadcast_to(pb[m : m + 1], (4, lanes)),
                ],
                axis=0,
            )
            corners.append(
                jnp.take_along_axis(table, picks, axis=1, mode="promise_in_bounds")
            )
        edge_one = corners[1] - corners[0]
        edge_two = corners[2] - corners[0]
        cross = edge_one * pltpu.roll(edge_two, 7, 0) - pltpu.roll(edge_one, 7, 0) * edge_two
        squares = cross * cross
        area = squares + pltpu.roll(squares, 7, 0) + pltpu.roll(squares, 6, 0)
        weight = jnp.sqrt(area + area_floor) / 6.0
        for s in range(3):
            others = [corners[m] for m in range(3) if m != s]
            points[p, s] = (2.0 / 3.0) * corners[s] + (1.0 / 6.0) * (others[0] + others[1])
        points[p, 3] = weight
        firsts = [points[p, s] for s in range(3)]
        head = jnp.concatenate([firsts[0][0:3], firsts[1][0:3], firsts[2][0:2]], axis=0)
        head_parts, tail_parts = three_parts(head), three_parts(firsts[2])
        first_rows[pl.ds(pl.multiple_of(32 * p, 32), 32), :] = jnp.concatenate(
            head_parts + [part[2:3] for part in tail_parts] + [jnp.zeros((5, lanes), f32)], axis=0
        )

    def points_step(h, carry):
        for u in range(4):
            make_points(4 * h + u)
        return carry

    lax.fori_loop(0, near // 4, points_step, 0)

    def turn_points(g, carry):
        rows = first_rows[pl.ds(pl.multiple_of(lanes * g, lanes), lanes), :]
        first_cols[g] = rows.T.astype(bf16)
        return carry

    lax.fori_loop(0, near // 4, turn_points, 0)

    chunk = 16

    def spread_first(p, target):
        target[...] = jnp.dot(first_cols[p // 4], picker[p % 4], preferred_element_type=f32)

    def make_block(p, cols, target, at):
        for c in range(lanes // chunk):
            at_rows = pl.ds(c * chunk, chunk)
            inv_sum = jnp.zeros((chunk, lanes), f32)
            cube_sum = jnp.zeros((chunk, lanes), f32)
            outer = [jnp.zeros((chunk, lanes), f32) for _ in range(5)]
            for s in range(3):
                a = [cols[at_rows, pl.ds((3 * s + i) * lanes, lanes)] for i in range(3)]
                for t in range(3):
                    d = [a[i] - points[p, t, 4 + i : 5 + i, :] for i in range(3)]
                    inv = lax.rsqrt(d[0] * d[0] + d[1] * d[1] + (d[2] * d[2] + soft_sq))
                    cube = inv * inv * inv
                    e0 = cube * d[0]
                    e1 = cube * d[1]
                    inv_sum = inv_sum + inv
                    cube_sum = cube_sum + cube
                    outer = [
                        outer[0] + e0 * d[0],
                        outer[1] + e0 * d[1],
                        outer[2] + e0 * d[2],
                        outer[3] + e1 * d[1],
                        outer[4] + e1 * d[2],
                    ]
            last = inv_sum - soft_sq * cube_sum - outer[0] - outer[3]
            diag = kelvin_diag * inv_sum
            entries = (
                outer[0] + diag,
                outer[1],
                outer[2],
                outer[3] + diag,
                outer[4],
                last + diag,
            )
            for q in range(6):
                value = entries[q]
                high = value.astype(bf16)
                at_lanes = pl.ds(q * lanes, lanes)
                target[at, at_rows, at_lanes] = high
                target[at, pl.ds(lanes + c * chunk, chunk), at_lanes] = (
                    value - high.astype(f32)
                ).astype(bf16)

    quarter = near // 4

    def make_quarter(k, recv):
        def step(h, carry):
            at = 2 * h
            p = k * quarter + at
            spread_first(p + 1, cols_odd)
            if recv is not None:
                near_pair(recv, p - quarter, blocks[k - 1], at)
            make_block(p, cols_even, blocks[k], at)
            spread_first(jnp.minimum(p + 2, near - 1), cols_even)
            if recv is not None:
                near_pair(recv, p + 1 - quarter, blocks[k - 1], at + 1)
            make_block(p + 1, cols_odd, blocks[k], at + 1)
            return carry

        lax.fori_loop(0, quarter // 2, step, 0)

    def apply_far(recv, base):
        def one(f):
            owner_a, rank_a = entry_slot(1, f)
            owner_b, rank_b = entry_slot(1, far + f)
            xa = recv[owner_a, base + rank_a]
            xb = recv[owner_b, base + rank_b]
            left = [left_ref[f, :, pl.ds(c * lanes, lanes)] for c in range(3)]
            right = [right_ref[f, :, pl.ds(c * lanes, lanes)] for c in range(3)]
            coef_b = jnp.sum(
                right[0] * xb[0:1] + right[1] * xb[1:2] + right[2] * xb[2:3], axis=1, keepdims=True
            )
            coef_a = jnp.sum(
                left[0] * xa[0:1] + left[1] * xa[1:2] + left[2] * xa[2:3], axis=1, keepdims=True
            )
            for c in range(3):
                far_terms[pl.ds(8 * f + c, 1), :] = jnp.sum(left[c] * coef_b, axis=0, keepdims=True)
                far_terms[pl.ds(8 * f + 4 + c, 1), :] = jnp.sum(
                    right[c] * coef_a, axis=0, keepdims=True
                )

        def step(h, carry):
            for u in range(4):
                one(4 * h + u)
            return carry

        lax.fori_loop(0, far // 4, step, 0)

    places = (
        ((0, 0),),
        ((0, 1), (1, 0)),
        ((0, 2), (2, 0)),
        ((1, 1),),
        ((1, 2), (2, 1)),
        ((2, 2),),
    )
    sub_id = lax.broadcasted_iota(i32, (8, lanes), 0)
    comp = sub_id % 4

    def spread_density(rows):
        split = []
        for i in range(3):
            row = rows[i : i + 1]
            high = row.astype(bf16).astype(f32)
            split.append(jnp.where(sub_id < 4, high, row - high))
        empty = jnp.zeros((8, lanes), f32)
        out = []
        for place in places:
            value = empty
            for r, i in place:
                value = jnp.where(comp == r, split[i], value)
            out.append(jnp.concatenate([value, empty], axis=0).astype(bf16))
        return out

    def near_pair(recv, p, block, at):
        owner_a, rank_a = entry_slot(0, p)
        owner_b, rank_b = entry_slot(0, near + p)
        weight_a = points[p, 3, 0:1, :]
        weight_b = points[p, 3, 4:5, :]
        a = spread_density(recv[owner_a, rank_a] * weight_a)
        b = spread_density(recv[owner_b, rank_b] * weight_b)
        into_b = jnp.zeros((8, lanes), f32)
        for q in range(6):
            into_b = into_b + jnp.dot(
                jnp.concatenate([a[q], a[q]], axis=1),
                block[at, :, pl.ds(q * lanes, lanes)],
                preferred_element_type=f32,
            )[0:8]
        back = lax.dot_general(
            jnp.concatenate(b, axis=1),
            block[at],
            (((1,), (1,)), ((), ())),
            preferred_element_type=f32,
        )
        into_a = back[0:8, :lanes] + back[0:8, lanes:]
        into_a = (into_a + pltpu.roll(into_a, 4, 0)) * weight_a
        into_b = (into_b + pltpu.roll(into_b, 4, 0)) * weight_b
        near_terms[pl.ds(pl.multiple_of(8 * p, 8), 8), :] = jnp.where(sub_id < 4, into_a, into_b)

    def apply_quarter(k, recv):
        def step(h, carry):
            for u in range(4):
                near_pair(recv, k * quarter + 4 * h + u, blocks[k], 4 * h + u)
            return carry

        lax.fori_loop(0, quarter // 4, step, 0)

    def fill_terms(send, source, row):
        def fill(o):
            for k in range(2):
                entry = jnp.clip(tab_s[row + k, o], 0, lanes)
                send[o, k] = source[pl.ds(4 * entry, 3), :]

        return fill

    def reduce_terms(stage, target, here):
        for c in range(3):
            total = jnp.zeros((clusters, lanes), f32)
            for k in range(2):
                total = total + jnp.dot(
                    one_hot[k, :, pl.ds(0, n)],
                    near_recv[stage, :, k, c, :],
                    precision=highest,
                    preferred_element_type=f32,
                )
                total = total + jnp.dot(
                    one_hot[2 + k, :, pl.ds(0, n)],
                    far_recv[stage, :, k, c, :],
                    precision=highest,
                    preferred_element_type=f32,
                )
            target[c] = total
            if here is not None:
                here[:, c, :] = total

    def mean_of(u, v):
        return jnp.sum(jnp.sum(u * v, axis=0), keepdims=True) * (1.0 / size_all)

    def send_sums(which, values):
        lane_row = lax.broadcasted_iota(i32, (1, lanes), 1)
        row = jnp.zeros((1, lanes), f32)
        for j, value in enumerate(values):
            row = jnp.where(lane_row == j, value, row)
        sum_send[which] = row
        pltpu.make_async_copy(
            sum_send.at[which], sum_recv.at[which, me], recv_sem.at[7 + which]
        ).start()

        def step(i, carry):
            peer = lax.rem(me + i, n)
            pltpu.make_async_remote_copy(
                sum_send.at[which],
                sum_recv.at[which, me],
                send_sem.at[7 + which],
                recv_sem.at[7 + which],
                device_id=(peer,),
                device_id_type=mesh_id,
            ).start()
            return carry

        lax.fori_loop(1, n, step, 0)

    def take_sums(which, count):
        arrived(sum_recv.at[which], 7 + which)
        total = jnp.sum(sum_recv[which], axis=0)
        return [total[0:1, j : j + 1] for j in range(count)]

    spread_first(0, cols_even)
    make_quarter(0, None)
    arrived(x_recv, 2)
    apply_far(x_recv, 2)
    exchange(far_send.at[0], far_recv.at[0], 3, fill_terms(far_send.at[0], far_terms, 4))
    for k in range(1, 4):
        make_quarter(k, x_recv)
    apply_quarter(3, x_recv)
    exchange(near_send.at[0], near_recv.at[0], 4, fill_terms(near_send.at[0], near_terms, 2))
    arrived(far_recv.at[0], 3)
    arrived(near_recv.at[0], 4)
    reduce_terms(0, y_all, y_here)

    exchange(yn_send, yn_recv, 9, fill_density(yn_send, y_here, (0, 1)))
    exchange(yf_send, yf_recv, 10, fill_density(yf_send, y_here, (2, 3)))
    x = x_ref[...]
    y = y_all[...]
    send_sums(0, [mean_of(x, x), mean_of(x, y), mean_of(y, y)])
    arrived(yn_recv, 9)
    apply_quarter(0, yn_recv)
    apply_quarter(1, yn_recv)
    arrived(yf_recv, 10)
    apply_far(yf_recv, 0)
    exchange(far_send.at[1], far_recv.at[1], 5, fill_terms(far_send.at[1], far_terms, 4))
    apply_quarter(2, yn_recv)
    apply_quarter(3, yn_recv)
    exchange(near_send.at[1], near_recv.at[1], 6, fill_terms(near_send.at[1], near_terms, 2))
    xx, xy, yy = take_sums(0, 3)
    scale_sq = xx + norm_eps
    scale = jnp.sqrt(scale_sq)
    proj_first = xy / scale_sq
    resid_sq = (yy - proj_first * xy * (1.0 + norm_eps / scale_sq)) / scale_sq
    norm_sq = resid_sq + norm_eps
    norm_first = jnp.sqrt(norm_sq)
    shrink = 1.0 / (scale * norm_first)
    x = x_ref[...]
    y = y_all[...]
    basis_one = x / scale
    basis_two = (y - proj_first * x) * shrink
    basis_ref[0] = basis_two
    arrived(far_recv.at[1], 5)
    arrived(near_recv.at[1], 6)
    reduce_terms(1, z_all, None)
    image_two = (z_all[...] - proj_first * y_all[...]) * shrink
    send_sums(
        1, [mean_of(basis_one, image_two), mean_of(basis_two, image_two), mean_of(image_two, image_two)]
    )
    cross, second, image_sq = take_sums(1, 3)
    one_sq = xx / scale_sq
    two_sq = resid_sq / norm_sq
    one_two = xy * norm_eps / (scale_sq * scale_sq * norm_first)
    last_sq = (
        image_sq
        + cross * cross * (one_sq - 2.0)
        + second * second * (two_sq - 2.0)
        + 2.0 * cross * second * one_two
    )
    norm_second = jnp.sqrt(last_sq + norm_eps)
    shrink_two = 1.0 / norm_second
    basis_ref[1] = (image_two - cross * basis_one - second * basis_two) * shrink_two
    row_id = lax.broadcasted_iota(i32, (2, 3), 1)
    col_id = lax.broadcasted_iota(i32, (2, 3), 0)
    hess = jnp.zeros((2, 3), f32)
    placed = (
        (0, 0, proj_first),
        (0, 1, cross),
        (1, 0, norm_first),
        (1, 1, second),
        (2, 1, norm_second),
    )
    for r, c, value in placed:
        hess = jnp.where((row_id == r) & (col_id == c), value, hess)
    hess_ref[...] = hess

    sent(req_send, 0)
    sent(geo_send, 1)
    sent(x_send, 2)
    sent(far_send.at[0], 3)
    sent(near_send.at[0], 4)
    sent(far_send.at[1], 5)
    sent(near_send.at[1], 6)
    sent(yn_send, 9)
    sent(yf_send, 10)
    for which in range(2):
        sent(sum_recv.at[which], 7 + which)


def per_device(
    right_side, vertices, panels, near_owner, near_local, far_owner, far_local, far_left, far_right
):
    n = lax.axis_size("dev")
    near = near_owner.shape[0]
    far = far_owner.shape[0]
    clusters = right_side.shape[0]

    vmem = pltpu.VMEM
    basis, hess = pl.pallas_call(
        functools.partial(kernel, n, near, far),
        out_shape=(
            jax.ShapeDtypeStruct((2, 3, clusters, lanes), f32),
            jax.ShapeDtypeStruct((2, 3), f32),
        ),
        in_specs=[pl.BlockSpec(memory_space=vmem)] * 9,
        out_specs=(pl.BlockSpec(memory_space=vmem),) * 2,
        scratch_shapes=[
            vmem((n, 1, lanes), f32),
            vmem((n, 1, lanes), f32),
            vmem((8, lanes), i32),
            pltpu.SMEM((8, lanes), i32),
            vmem((8, lanes), i32),
            pltpu.SMEM((8, lanes), i32),
            vmem((4, clusters, lanes), f32),
            vmem((clusters, 3, lanes), f32),
            vmem((clusters, 3, lanes), f32),
            vmem((clusters, 3, lanes), f32),
            vmem((n, 2, 2, 3, lanes), f32),
            vmem((n, 2, 2, 3, lanes), f32),
            vmem((n, 4, 3, lanes), f32),
            vmem((n, 4, 3, lanes), f32),
            vmem((n, 2, 3, lanes), f32),
            vmem((n, 2, 3, lanes), f32),
            vmem((n, 2, 3, lanes), f32),
            vmem((n, 2, 3, lanes), f32),
            vmem((2, n, 2, 3, lanes), f32),
            vmem((2, n, 2, 3, lanes), f32),
            vmem((2, n, 2, 3, lanes), f32),
            vmem((2, n, 2, 3, lanes), f32),
            vmem((near, 4, 8, lanes), f32),
            vmem((32 * near, lanes), f32),
            vmem((near // 4, lanes, lanes), bf16),
            vmem((4, lanes, 9 * lanes), bf16),
            vmem((lanes, 9 * lanes), f32),
            vmem((lanes, 9 * lanes), f32),
            vmem((near // 4, 2 * lanes, 6 * lanes), bf16),
            vmem((near // 4, 2 * lanes, 6 * lanes), bf16),
            vmem((near // 4, 2 * lanes, 6 * lanes), bf16),
            vmem((near // 4, 2 * lanes, 6 * lanes), bf16),
            vmem((4 * lanes + 8, lanes), f32),
            vmem((4 * lanes + 8, lanes), f32),
            vmem((3, clusters, lanes), f32),
            vmem((3, clusters, lanes), f32),
            vmem((clusters, 3, lanes), f32),
            vmem((2, 1, lanes), f32),
            vmem((2, n, 1, lanes), f32),
            pltpu.SemaphoreType.DMA((11,)),
            pltpu.SemaphoreType.DMA((11,)),
            pltpu.SemaphoreType.DMA((2,)),
        ],
        compiler_params=pltpu.CompilerParams(
            collective_id=0, has_side_effects=True, vmem_limit_bytes=58 * 1024 * 1024
        ),
    )(
        near_owner.T,
        near_local.T,
        far_owner.T,
        far_local.T,
        right_side.transpose(1, 0, 2),
        vertices.transpose(1, 0, 2),
        panels.transpose(1, 0, 2),
        far_left,
        far_right,
    )
    return basis.transpose(0, 2, 1, 3), hess.T


def solution(mesh):
    block = P("dev", None, None)
    pair = P("dev", None)
    return jax.shard_map(
        per_device,
        mesh=mesh,
        in_specs=(block, block, block, pair, pair, pair, pair, block, block),
        out_specs=(P(None, "dev", None, None), P()),
        check_vma=False,
    )
```

time: 244 us -> 158 us (0.65)
  Pallas kernels: 232 us -> 155 us
  local copies, waits for them, and re-layouts: 11.4 us -> 2.8 us
    pallas_call x1, Pallas kernels: 232 us -> 155 us  [per_device(): pl.pallas_call(functools.partial(kernel, n, near, far), out_shape=(jax.Sh...]
    reshape x4 -> x0, local copies, waits for them, and re-layouts: 3.04 us -> none  [entry_row(): row = table.T.reshape(1, -1)]
    pallas_call x2 -> x0, local copies, waits for them, and re-layouts: 2.95 us -> none  [per_device(): pl.pallas_call(functools.partial(kernel, n, near, far), out_shape=(jax.Sh...]
where the time goes in v2:
time: 158 us
  Pallas kernels  155 us (98%)
  local copies, waits for them, and re-layouts  2.8 us (2%)
    pallas_call x1, Pallas kernels, per_device(): pl.pallas_call(functools.partial(kernel, n, near, far), out_shape=(jax.Sh...  155 us

profile of v2, /device:TPU:1, one launch (start us, length us, event | category | flops | bytes accessed | tf_op | source)
XLA Modules:
  0.0 158.0 jit_solution(3157421401461590728)
XLA Ops:
  0.6 154.5 %shard_map.104 = (f32[2,3,64,128]{3,2,1,0:T(8,128)}, f32[2,3]{1,0:T(2,128)}) custom-call(s32[2,64]{1,0:T(2,128)} %bitcast.13, s32[2,64]{1,0:T(2,128)} %bitcast.14, s32[2,64]{1,0:T(2,128)} %bitcast.15, s32[2,64]{1,0:T(2,128)} %bitcast.16, f32[3,64,128]{2,1,0:T(8,128)} %bitcast.10, f32[3,64,128]{2,1,0:T(8,128)} %bitcast.11, s32[3,64,128]{2,1,0:T(8,128)} %bitcast.12, ...), custom_call_target="tpu_custom_call" | custom-call | tf_op jit(solution)/shard_map/pallas_call | solution.py:577
  155.2 1.6 %copy.13 = f32[2,64,3,128]{3,1,2,0:T(8,128)} copy(f32[2,64,3,128]{3,1,2,0:T(8,128)} %bitcast.9) | data formatting | bytes 393216
  156.8 1.2 copy.14

commit v3 on v2

--- a/solution.py
+++ b/solution.py
@@ -116,13 +116,23 @@
 
     barrier = pltpu.get_barrier_semaphore()
 
-    def greet(i, carry):
-        pl.semaphore_signal(
-            barrier, inc=1, device_id=(lax.rem(me + i, n),), device_id_type=mesh_id
-        )
-        return carry
-
-    lax.fori_loop(1, n, greet, 0)
+    def every_peer(body):
+        group = 4
+        count = (n - 1) // group
+
+        def step(g, carry):
+            for u in range(group):
+                body(lax.rem(me + (1 + group * g + u), n))
+            return carry
+
+        lax.fori_loop(0, count, step, 0)
+        for i in range(1 + group * count, n):
+            body(lax.rem(me + i, n))
+
+    def greet(peer):
+        pl.semaphore_signal(barrier, inc=1, device_id=(peer,), device_id_type=mesh_id)
+
+    every_peer(greet)
 
     def asked_id(k, o):
         return jnp.clip(ask_s[k, o], 0, clusters - 1)
@@ -139,6 +149,33 @@
     to_smem.start()
     req_rows = jnp.concatenate(near_req + far_req + [jnp.zeros((lanes - 4, lanes), f32)], axis=0)
     req_send[...] = req_rows.T[:n].reshape(n, 1, lanes)
+    pl.semaphore_wait(barrier, n - 1)
+
+    def exchange(send, recv, which, fill):
+        fill(me)
+        pltpu.make_async_copy(send.at[me], recv.at[me], recv_sem.at[which]).start()
+
+        def step(peer):
+            fill(peer)
+            pltpu.make_async_remote_copy(
+                send.at[peer],
+                recv.at[me],
+                send_sem.at[which],
+                recv_sem.at[which],
+                device_id=(peer,),
+                device_id_type=mesh_id,
+            ).start()
+
+        every_peer(step)
+
+    def arrived(recv, which):
+        pltpu.make_async_copy(recv, recv, recv_sem.at[which]).wait()
+
+    def sent(send, which):
+        part = send.at[pl.ds(0, n - 1)]
+        pltpu.make_async_copy(part, part, send_sem.at[which]).wait()
+
+    exchange(req_send, req_recv, 0, lambda o: None)
     for c in range(3):
         x_here[:, c, :] = x_ref[c]
         vert_here[:, c, :] = vert_ref[c]
@@ -156,35 +193,6 @@
                 hit = (place >= 24) & (place < 27)
             picker[r, :, pl.ds(j * lanes, lanes)] = jnp.where(hit, 1.0, 0.0).astype(bf16)
 
-    pl.semaphore_wait(barrier, n - 1)
-
-    def exchange(send, recv, which, fill):
-        fill(me)
-        pltpu.make_async_copy(send.at[me], recv.at[me], recv_sem.at[which]).start()
-
-        def step(i, carry):
-            peer = lax.rem(me + i, n)
-            fill(peer)
-            pltpu.make_async_remote_copy(
-                send.at[peer],
-                recv.at[me],
-                send_sem.at[which],
-                recv_sem.at[which],
-                device_id=(peer,),
-                device_id_type=mesh_id,
-            ).start()
-            return carry
-
-        lax.fori_loop(1, n, step, 0)
-
-    def arrived(recv, which):
-        pltpu.make_async_copy(recv, recv, recv_sem.at[which]).wait()
-
-    def sent(send, which):
-        part = send.at[pl.ds(0, n - 1)]
-        pltpu.make_async_copy(part, part, send_sem.at[which]).wait()
-
-    exchange(req_send, req_recv, 0, lambda o: None)
     arrived(req_recv, 0)
     asked = req_recv[...].reshape(n, lanes)
     if n < lanes:
@@ -459,8 +467,7 @@
             sum_send.at[which], sum_recv.at[which, me], recv_sem.at[7 + which]
         ).start()
 
-        def step(i, carry):
-            peer = lax.rem(me + i, n)
+        def step(peer):
             pltpu.make_async_remote_copy(
                 sum_send.at[which],
                 sum_recv.at[which, me],
@@ -469,9 +476,8 @@
                 device_id=(peer,),
                 device_id_type=mesh_id,
             ).start()
-            return carry
-
-        lax.fori_loop(1, n, step, 0)
+
+        every_peer(step)
 
     def take_sums(which, count):
         arrived(sum_recv.at[which], 7 + which)
@@ -624,7 +630,7 @@
             vmem((2, n, 1, lanes), f32),
             pltpu.SemaphoreType.DMA((11,)),
             pltpu.SemaphoreType.DMA((11,)),
-            pltpu.SemaphoreType.DMA((2,)),
+            pltpu.SemaphoreType.DMA((4,)),
         ],
         compiler_params=pltpu.CompilerParams(
             collective_id=0, has_side_effects=True, vmem_limit_bytes=58 * 1024 * 1024

time: 158 us -> 156 us (0.987)
  Pallas kernels: 155 us -> 153 us
    pallas_call x1, Pallas kernels: 155 us -> 153 us  [per_device(): pl.pallas_call(functools.partial(kernel, n, near, far), out_shape=(jax.Sh...]
where the time goes in v3:
time: 156 us
  Pallas kernels  153 us (98%)
  local copies, waits for them, and re-layouts  2.8 us (2%)
    pallas_call x1, Pallas kernels, per_device(): pl.pallas_call(functools.partial(kernel, n, near, far), out_shape=(jax.Sh...  153 us

profile of v3, /device:TPU:1, one launch (start us, length us, event | category | flops | bytes accessed | tf_op | source)
XLA Modules:
  0.0 156.1 jit_solution(9496803168383589541)
XLA Ops:
  0.6 152.7 %shard_map.104 = (f32[2,3,64,128]{3,2,1,0:T(8,128)}, f32[2,3]{1,0:T(2,128)}) custom-call(s32[2,64]{1,0:T(2,128)} %bitcast.13, s32[2,64]{1,0:T(2,128)} %bitcast.14, s32[2,64]{1,0:T(2,128)} %bitcast.15, s32[2,64]{1,0:T(2,128)} %bitcast.16, f32[3,64,128]{2,1,0:T(8,128)} %bitcast.10, f32[3,64,128]{2,1,0:T(8,128)} %bitcast.11, s32[3,64,128]{2,1,0:T(8,128)} %bitcast.12, ...), custom_call_target="tpu_custom_call" | custom-call | tf_op jit(solution)/shard_map/pallas_call | solution.py:583
  153.3 1.6 %copy.13 = f32[2,64,3,128]{3,1,2,0:T(8,128)} copy(f32[2,64,3,128]{3,1,2,0:T(8,128)} %bitcast.9) | data formatting | bytes 393216
  155.0 1.2 copy.14

commit v4 on v3

--- a/solution.py
+++ b/solution.py
@@ -105,6 +105,8 @@
     y_here,
     sum_send,
     sum_recv,
+    inner_recv,
+    outer_recv,
     send_sem,
     recv_sem,
     local_sem,
@@ -171,8 +173,8 @@
     def arrived(recv, which):
         pltpu.make_async_copy(recv, recv, recv_sem.at[which]).wait()
 
-    def sent(send, which):
-        part = send.at[pl.ds(0, n - 1)]
+    def sent(send, which, count=n):
+        part = send.at[pl.ds(0, count - 1)]
         pltpu.make_async_copy(part, part, send_sem.at[which]).wait()
 
     exchange(req_send, req_recv, 0, lambda o: None)
@@ -434,22 +436,24 @@
 
         return fill
 
-    def reduce_terms(stage, target, here):
+    def gathered(recv, stage, first, c):
+        total = jnp.zeros((clusters, lanes), f32)
+        for k in range(2):
+            total = total + jnp.dot(
+                one_hot[first + k, :, pl.ds(0, n)],
+                recv[stage, :, k, c, :],
+                precision=highest,
+                preferred_element_type=f32,
+            )
+        return total
+
+    def reduce_near(stage, target):
         for c in range(3):
-            total = jnp.zeros((clusters, lanes), f32)
-            for k in range(2):
-                total = total + jnp.dot(
-                    one_hot[k, :, pl.ds(0, n)],
-                    near_recv[stage, :, k, c, :],
-                    precision=highest,
-                    preferred_element_type=f32,
-                )
-                total = total + jnp.dot(
-                    one_hot[2 + k, :, pl.ds(0, n)],
-                    far_recv[stage, :, k, c, :],
-                    precision=highest,
-                    preferred_element_type=f32,
-                )
+            target[c] = gathered(near_recv, stage, 0, c)
+
+    def reduce_far(stage, target, here):
+        for c in range(3):
+            total = target[c] + gathered(far_recv, stage, 2, c)
             target[c] = total
             if here is not None:
                 here[:, c, :] = total
@@ -457,61 +461,92 @@
     def mean_of(u, v):
         return jnp.sum(jnp.sum(u * v, axis=0), keepdims=True) * (1.0 / size_all)
 
-    def send_sums(which, values):
+    def row_of(values):
         lane_row = lax.broadcasted_iota(i32, (1, lanes), 1)
         row = jnp.zeros((1, lanes), f32)
         for j, value in enumerate(values):
             row = jnp.where(lane_row == j, value, row)
-        sum_send[which] = row
-        pltpu.make_async_copy(
-            sum_send.at[which], sum_recv.at[which, me], recv_sem.at[7 + which]
-        ).start()
+        return row
+
+    def send_sums(values):
+        sum_send[0] = row_of(values)
+        pltpu.make_async_copy(sum_send.at[0], sum_recv.at[me], recv_sem.at[7]).start()
 
         def step(peer):
             pltpu.make_async_remote_copy(
-                sum_send.at[which],
-                sum_recv.at[which, me],
-                send_sem.at[7 + which],
-                recv_sem.at[7 + which],
+                sum_send.at[0],
+                sum_recv.at[me],
+                send_sem.at[7],
+                recv_sem.at[7],
                 device_id=(peer,),
                 device_id_type=mesh_id,
             ).start()
 
         every_peer(step)
 
-    def take_sums(which, count):
-        arrived(sum_recv.at[which], 7 + which)
-        total = jnp.sum(sum_recv[which], axis=0)
+    def take_sums(count):
+        arrived(sum_recv, 7)
+        total = jnp.sum(sum_recv[...], axis=0)
         return [total[0:1, j : j + 1] for j in range(count)]
+
+    inner = 16
+    outer = n // inner
+    position = lax.rem(me, inner)
+    group = lax.div(me, inner)
+
+    def group_sum(row, slot, recv, which, own, size, device):
+        sum_send[slot] = row
+        pltpu.make_async_copy(sum_send.at[slot], recv.at[own], recv_sem.at[which]).start()
+        for u in range(1, size):
+            pltpu.make_async_remote_copy(
+                sum_send.at[slot],
+                recv.at[own],
+                send_sem.at[which],
+                recv_sem.at[which],
+                device_id=(device(lax.rem(own + u, size)),),
+                device_id_type=mesh_id,
+            ).start()
+        arrived(recv, which)
+        return jnp.sum(recv[...], axis=0)
+
+    def sum_everywhere(values):
+        part = group_sum(
+            row_of(values), 1, inner_recv, 8, position, inner, lambda i: group * inner + i
+        )
+        total = group_sum(
+            part, 2, outer_recv, 11, group, outer, lambda i: i * inner + position
+        )
+        return [total[0:1, j : j + 1] for j in range(len(values))]
 
     spread_first(0, cols_even)
     make_quarter(0, None)
     arrived(x_recv, 2)
-    apply_far(x_recv, 2)
-    exchange(far_send.at[0], far_recv.at[0], 3, fill_terms(far_send.at[0], far_terms, 4))
     for k in range(1, 4):
         make_quarter(k, x_recv)
     apply_quarter(3, x_recv)
     exchange(near_send.at[0], near_recv.at[0], 4, fill_terms(near_send.at[0], near_terms, 2))
+    apply_far(x_recv, 2)
+    exchange(far_send.at[0], far_recv.at[0], 3, fill_terms(far_send.at[0], far_terms, 4))
+    arrived(near_recv.at[0], 4)
+    reduce_near(0, y_all)
     arrived(far_recv.at[0], 3)
-    arrived(near_recv.at[0], 4)
-    reduce_terms(0, y_all, y_here)
+    reduce_far(0, y_all, y_here)
 
     exchange(yn_send, yn_recv, 9, fill_density(yn_send, y_here, (0, 1)))
     exchange(yf_send, yf_recv, 10, fill_density(yf_send, y_here, (2, 3)))
     x = x_ref[...]
     y = y_all[...]
-    send_sums(0, [mean_of(x, x), mean_of(x, y), mean_of(y, y)])
+    send_sums([mean_of(x, x), mean_of(x, y), mean_of(y, y)])
     arrived(yn_recv, 9)
     apply_quarter(0, yn_recv)
     apply_quarter(1, yn_recv)
+    apply_quarter(2, yn_recv)
+    apply_quarter(3, yn_recv)
+    exchange(near_send.at[1], near_recv.at[1], 6, fill_terms(near_send.at[1], near_terms, 2))
     arrived(yf_recv, 10)
     apply_far(yf_recv, 0)
     exchange(far_send.at[1], far_recv.at[1], 5, fill_terms(far_send.at[1], far_terms, 4))
-    apply_quarter(2, yn_recv)
-    apply_quarter(3, yn_recv)
-    exchange(near_send.at[1], near_recv.at[1], 6, fill_terms(near_send.at[1], near_terms, 2))
-    xx, xy, yy = take_sums(0, 3)
+    xx, xy, yy = take_sums(3)
     scale_sq = xx + norm_eps
     scale = jnp.sqrt(scale_sq)
     proj_first = xy / scale_sq
@@ -524,14 +559,14 @@
     basis_one = x / scale
     basis_two = (y - proj_first * x) * shrink
     basis_ref[0] = basis_two
+    arrived(near_recv.at[1], 6)
+    reduce_near(1, z_all)
     arrived(far_recv.at[1], 5)
-    arrived(near_recv.at[1], 6)
-    reduce_terms(1, z_all, None)
+    reduce_far(1, z_all, None)
     image_two = (z_all[...] - proj_first * y_all[...]) * shrink
-    send_sums(
-        1, [mean_of(basis_one, image_two), mean_of(basis_two, image_two), mean_of(image_two, image_two)]
+    cross, second, image_sq = sum_everywhere(
+        [mean_of(basis_one, image_two), mean_of(basis_two, image_two), mean_of(image_two, image_two)]
     )
-    cross, second, image_sq = take_sums(1, 3)
     one_sq = xx / scale_sq
     two_sq = resid_sq / norm_sq
     one_two = xy * norm_eps / (scale_sq * scale_sq * norm_first)
@@ -567,8 +602,9 @@
     sent(near_send.at[1], 6)
     sent(yn_send, 9)
     sent(yf_send, 10)
-    for which in range(2):
-        sent(sum_recv.at[which], 7 + which)
+    sent(sum_recv, 7, n)
+    sent(inner_recv, 8, inner)
+    sent(outer_recv, 11, outer)
 
 
 def per_device(
@@ -626,10 +662,12 @@
             vmem((3, clusters, lanes), f32),
             vmem((3, clusters, lanes), f32),
             vmem((clusters, 3, lanes), f32),
-            vmem((2, 1, lanes), f32),
-            vmem((2, n, 1, lanes), f32),
-            pltpu.SemaphoreType.DMA((11,)),
-            pltpu.SemaphoreType.DMA((11,)),
+            vmem((3, 1, lanes), f32),
+            vmem((n, 1, lanes), f32),
+            vmem((16, 1, lanes), f32),
+            vmem((n // 16, 1, lanes), f32),
+            pltpu.SemaphoreType.DMA((12,)),
+            pltpu.SemaphoreType.DMA((12,)),
             pltpu.SemaphoreType.DMA((4,)),
         ],
         compiler_params=pltpu.CompilerParams(

time: 156 us -> 158 us (1.013)
    pallas_call x1, Pallas kernels: 153 us -> 154 us  [per_device(): pl.pallas_call(functools.partial(kernel, n, near, far), out_shape=(jax.Sh...]
where the time goes in v4:
time: 158 us
  Pallas kernels  154 us (97%)
  local copies, waits for them, and re-layouts  2.8 us (2%)
    pallas_call x1, Pallas kernels, per_device(): pl.pallas_call(functools.partial(kernel, n, near, far), out_shape=(jax.Sh...  154 us

profile of v4, /device:TPU:1, one launch (start us, length us, event | category | flops | bytes accessed | tf_op | source)
XLA Modules:
  0.0 157.9 jit_solution(11739339223128970421)
XLA Ops:
  0.6 154.5 %shard_map.104 = (f32[2,3,64,128]{3,2,1,0:T(8,128)}, f32[2,3]{1,0:T(2,128)}) custom-call(s32[2,64]{1,0:T(2,128)} %bitcast.13, s32[2,64]{1,0:T(2,128)} %bitcast.14, s32[2,64]{1,0:T(2,128)} %bitcast.15, s32[2,64]{1,0:T(2,128)} %bitcast.16, f32[3,64,128]{2,1,0:T(8,128)} %bitcast.10, f32[3,64,128]{2,1,0:T(8,128)} %bitcast.11, s32[3,64,128]{2,1,0:T(8,128)} %bitcast.12, ...), custom_call_target="tpu_custom_call" | custom-call | tf_op jit(solution)/shard_map/pallas_call | solution.py:619
  155.1 1.6 %copy.13 = f32[2,64,3,128]{3,1,2,0:T(8,128)} copy(f32[2,64,3,128]{3,1,2,0:T(8,128)} %bitcast.9) | data formatting | bytes 393216
  156.7 1.2 copy.14

commit v5 on v4

--- a/solution.py
+++ b/solution.py
@@ -62,10 +62,12 @@
     x_ref,
     vert_ref,
     panel_ref,
+    left_hbm,
+    right_hbm,
+    basis_ref,
+    hess_ref,
     left_ref,
     right_ref,
-    basis_ref,
-    hess_ref,
     req_send,
     req_recv,
     tab_v,
@@ -135,6 +137,10 @@
         pl.semaphore_signal(barrier, inc=1, device_id=(peer,), device_id_type=mesh_id)
 
     every_peer(greet)
+    left_copy = pltpu.make_async_copy(left_hbm, left_ref, local_sem.at[2])
+    right_copy = pltpu.make_async_copy(right_hbm, right_ref, local_sem.at[3])
+    left_copy.start()
+    right_copy.start()
 
     def asked_id(k, o):
         return jnp.clip(ask_s[k, o], 0, clusters - 1)
@@ -285,9 +291,7 @@
     def make_block(p, cols, target, at):
         for c in range(lanes // chunk):
             at_rows = pl.ds(c * chunk, chunk)
-            inv_sum = jnp.zeros((chunk, lanes), f32)
-            cube_sum = jnp.zeros((chunk, lanes), f32)
-            outer = [jnp.zeros((chunk, lanes), f32) for _ in range(5)]
+            sums = None
             for s in range(3):
                 a = [cols[at_rows, pl.ds((3 * s + i) * lanes, lanes)] for i in range(3)]
                 for t in range(3):
@@ -296,15 +300,12 @@
                     cube = inv * inv * inv
                     e0 = cube * d[0]
                     e1 = cube * d[1]
-                    inv_sum = inv_sum + inv
-                    cube_sum = cube_sum + cube
-                    outer = [
-                        outer[0] + e0 * d[0],
-                        outer[1] + e0 * d[1],
-                        outer[2] + e0 * d[2],
-                        outer[3] + e1 * d[1],
-                        outer[4] + e1 * d[2],
-                    ]
+                    terms = [inv, cube, e0 * d[0], e0 * d[1], e0 * d[2], e1 * d[1], e1 * d[2]]
+                    if sums is None:
+                        sums = terms
+                    else:
+                        sums = [total + term for total, term in zip(sums, terms)]
+            inv_sum, cube_sum, *outer = sums
             last = inv_sum - soft_sq * cube_sum - outer[0] - outer[3]
             diag = kelvin_diag * inv_sum
             entries = (
@@ -447,13 +448,13 @@
             )
         return total
 
-    def reduce_near(stage, target):
+    def reduce_far(stage, target):
         for c in range(3):
-            target[c] = gathered(near_recv, stage, 0, c)
-
-    def reduce_far(stage, target, here):
+            target[c] = gathered(far_recv, stage, 2, c)
+
+    def reduce_near(stage, target, here):
         for c in range(3):
-            total = target[c] + gathered(far_recv, stage, 2, c)
+            total = target[c] + gathered(near_recv, stage, 0, c)
             target[c] = total
             if here is not None:
                 here[:, c, :] = total
@@ -521,16 +522,18 @@
     spread_first(0, cols_even)
     make_quarter(0, None)
     arrived(x_recv, 2)
+    left_copy.wait()
+    right_copy.wait()
+    apply_far(x_recv, 2)
+    exchange(far_send.at[0], far_recv.at[0], 3, fill_terms(far_send.at[0], far_terms, 4))
     for k in range(1, 4):
         make_quarter(k, x_recv)
     apply_quarter(3, x_recv)
     exchange(near_send.at[0], near_recv.at[0], 4, fill_terms(near_send.at[0], near_terms, 2))
-    apply_far(x_recv, 2)
-    exchange(far_send.at[0], far_recv.at[0], 3, fill_terms(far_send.at[0], far_terms, 4))
+    arrived(far_recv.at[0], 3)
+    reduce_far(0, y_all)
     arrived(near_recv.at[0], 4)
-    reduce_near(0, y_all)
-    arrived(far_recv.at[0], 3)
-    reduce_far(0, y_all, y_here)
+    reduce_near(0, y_all, y_here)
 
     exchange(yn_send, yn_recv, 9, fill_density(yn_send, y_here, (0, 1)))
     exchange(yf_send, yf_recv, 10, fill_density(yf_send, y_here, (2, 3)))
@@ -540,12 +543,12 @@
     arrived(yn_recv, 9)
     apply_quarter(0, yn_recv)
     apply_quarter(1, yn_recv)
+    arrived(yf_recv, 10)
+    apply_far(yf_recv, 0)
+    exchange(far_send.at[1], far_recv.at[1], 5, fill_terms(far_send.at[1], far_terms, 4))
     apply_quarter(2, yn_recv)
     apply_quarter(3, yn_recv)
     exchange(near_send.at[1], near_recv.at[1], 6, fill_terms(near_send.at[1], near_terms, 2))
-    arrived(yf_recv, 10)
-    apply_far(yf_recv, 0)
-    exchange(far_send.at[1], far_recv.at[1], 5, fill_terms(far_send.at[1], far_terms, 4))
     xx, xy, yy = take_sums(3)
     scale_sq = xx + norm_eps
     scale = jnp.sqrt(scale_sq)
@@ -559,10 +562,10 @@
     basis_one = x / scale
     basis_two = (y - proj_first * x) * shrink
     basis_ref[0] = basis_two
+    arrived(far_recv.at[1], 5)
+    reduce_far(1, z_all)
     arrived(near_recv.at[1], 6)
-    reduce_near(1, z_all)
-    arrived(far_recv.at[1], 5)
-    reduce_far(1, z_all, None)
+    reduce_near(1, z_all, None)
     image_two = (z_all[...] - proj_first * y_all[...]) * shrink
     cross, second, image_sq = sum_everywhere(
         [mean_of(basis_one, image_two), mean_of(basis_two, image_two), mean_of(image_two, image_two)]
@@ -622,9 +625,12 @@
             jax.ShapeDtypeStruct((2, 3, clusters, lanes), f32),
             jax.ShapeDtypeStruct((2, 3), f32),
         ),
-        in_specs=[pl.BlockSpec(memory_space=vmem)] * 9,
+        in_specs=[pl.BlockSpec(memory_space=vmem)] * 7
+        + [pl.BlockSpec(memory_space=pl.ANY)] * 2,
         out_specs=(pl.BlockSpec(memory_space=vmem),) * 2,
         scratch_shapes=[
+            vmem(far_left.shape, f32),
+            vmem(far_right.shape, f32),
             vmem((n, 1, lanes), f32),
             vmem((n, 1, lanes), f32),
             vmem((8, lanes), i32),

time: 158 us -> 157 us (level)
  no operation moved by 1% of the time
where the time goes in v5:
time: 157 us
  Pallas kernels  153 us (97%)
  local copies, waits for them, and re-layouts  2.8 us (2%)
    pallas_call x1, Pallas kernels, per_device(): pl.pallas_call(functools.partial(kernel, n, near, far), out_shape=(jax.Sh...  153 us

profile of v5, /device:TPU:1, one launch (start us, length us, event | category | flops | bytes accessed | tf_op | source)
XLA Modules:
  0.0 156.8 jit_solution(7399237660514630825)
XLA Ops:
  0.6 153.4 %shard_map.104 = (f32[2,3,64,128]{3,2,1,0:T(8,128)}, f32[2,3]{1,0:T(2,128)}) custom-call(s32[2,64]{1,0:T(2,128)} %bitcast.13, s32[2,64]{1,0:T(2,128)} %bitcast.14, s32[2,64]{1,0:T(2,128)} %bitcast.15, s32[2,64]{1,0:T(2,128)} %bitcast.16, f32[3,64,128]{2,1,0:T(8,128)} %bitcast.10, f32[3,64,128]{2,1,0:T(8,128)} %bitcast.11, s32[3,64,128]{2,1,0:T(8,128)} %bitcast.12, ...), custom_call_target="tpu_custom_call" | custom-call | tf_op jit(solution)/shard_map/pallas_call | solution.py:622
  154.0 1.6 %copy.13 = f32[2,64,3,128]{3,1,2,0:T(8,128)} copy(f32[2,64,3,128]{3,1,2,0:T(8,128)} %bitcast.9) | data formatting | bytes 393216
  155.6 1.2 copy.14
